TPU v7x, 32 devices: a whole 2x2x4 slice. The times are simulated.
32 devices in a mesh: section: 2 (over x), chan: 4 (over z), batch: 4 (over y, core).
Axes of the slice: x: 2, y: 2, z: 4, core: 2. Of those that a mesh axis runs over, the one named last changes fastest.
Arguments:
- images: bfloat16 [2, 4, 4, 256, 1024], P('section', 'batch', 'chan'), may hold values from -12 to 12
- w_early: bfloat16 [1024, 2048], replicated, may hold values from -0.1875 to 0.1875
- gain_early: float32 [2048], replicated, may hold values from 0.5 to 1.5
- bias_early: float32 [2048], replicated, may hold values from -0.5 to 0.5
- w_late: bfloat16 [2048, 8192], P(None, 'chan'), may hold values from -0.125 to 0.125
- gain_late: float32 [8192], P('chan'), may hold values from 0.5 to 1.5
- bias_late: float32 [8192], P('chan'), may hold values from -0.5 to 0.5
- cotangent: bfloat16 [2, 16, 256, 8192], P('section', 'batch', None, 'chan'), may hold values from -6 to 6
Outputs:
- late_out: bfloat16 [2, 16, 256, 8192], P('section', 'batch', None, 'chan')
- grad_late: float32 [2048, 8192], P(None, 'chan')
- grad_early: float32 [1024, 2048], P(('section', 'chan', 'batch'))
All inputs are finite; a program needn't handle non-finite values.
Results may differ from a plain program's by a relative error of at most 0.024.
Values may be sent and summed in bfloat16 or wider, within the bound.
A program may use at most 192 MiB of HBM per device.

v0:
```python
import jax
import jax.numpy as jnp
from jax import lax
from jax.sharding import PartitionSpec as P


def smooth_gate(values):
    return values * jax.nn.sigmoid(values)


def smooth_slope(values):
    sig = jax.nn.sigmoid(values)
    return sig * (1.0 + values * (1.0 - sig))


def body(images, w_early, gain_early, bias_early, w_late, gain_late, bias_late, cotangent):
    micro, batch_one, img_dev, pixels, width_in = images.shape
    width_mid = w_early.shape[1]
    width_out = w_late.shape[1]
    chan_count = lax.axis_size("chan")
    batch_count = lax.axis_size("batch")
    flat_in = images.reshape(-1, width_in)
    early_raw = jnp.dot(flat_in, w_early, preferred_element_type=jnp.float32).astype(jnp.bfloat16)
    total_rows = flat_in.shape[0] * chan_count * batch_count
    raw_f = early_raw.astype(jnp.float32)
    sum_one, sum_two = lax.psum((jnp.sum(raw_f, 0), jnp.sum(raw_f * raw_f, 0)), ("chan", "batch"))
    mean_e = sum_one / total_rows
    rstd_e = lax.rsqrt(sum_two / total_rows - mean_e * mean_e + 1e-05)
    normed_e = (raw_f - mean_e) * rstd_e
    pre_e = normed_e * gain_early + bias_early
    act_local = smooth_gate(pre_e).astype(jnp.bfloat16).reshape(img_dev, pixels, width_mid)
    act_full = lax.all_gather(act_local, "chan", axis=0, tiled=True)
    act_rows = act_full.reshape(-1, width_mid)
    late = jnp.dot(act_rows, w_late, preferred_element_type=jnp.float32)
    late_rows = act_rows.shape[0] * batch_count
    late_one, late_two = lax.psum((jnp.sum(late, 0), jnp.sum(late * late, 0)), "batch")
    mean_l = late_one / late_rows
    rstd_l = lax.rsqrt(late_two / late_rows - mean_l * mean_l + 1e-05)
    normed_l = (late - mean_l) * rstd_l
    pre_l = normed_l * gain_late + bias_late
    late_out = smooth_gate(pre_l).astype(jnp.bfloat16).reshape(cotangent.shape)
    grad_y = cotangent.reshape(-1, width_out).astype(jnp.float32) * smooth_slope(pre_l)
    back_one, back_two = lax.psum((jnp.sum(grad_y, 0), jnp.sum(grad_y * normed_l, 0)), "batch")
    grad_h = (
        gain_late * rstd_l * (grad_y - back_one / late_rows - normed_l * (back_two / late_rows))
    ).astype(jnp.bfloat16)
    local_late = lax.dot_general(
        act_rows, grad_h, (((0,), (0,)), ((), ())), preferred_element_type=jnp.float32
    )
    grad_late = lax.psum(local_late.astype(jnp.bfloat16), ("section", "batch")).astype(jnp.float32)
    grad_cube = grad_h.reshape(-1, pixels, width_out)
    piece = grad_cube
    grad_act = lax.psum_scatter(
        jnp.einsum("ipl,al->ipa", piece, w_late, preferred_element_type=jnp.float32).astype(
            jnp.bfloat16
        ),
        "chan",
        scatter_dimension=0,
        tiled=True,
    ).astype(jnp.float32)
    grad_act = grad_act.reshape(-1, width_mid)
    grad_pre = grad_act * smooth_slope(pre_e)
    early_one, early_two = lax.psum(
        (jnp.sum(grad_pre, 0), jnp.sum(grad_pre * normed_e, 0)), ("chan", "batch")
    )
    grad_raw = (
        gain_early
        * rstd_e
        * (grad_pre - early_one / total_rows - normed_e * (early_two / total_rows))
    ).astype(jnp.bfloat16)
    piece = flat_in
    grad_early = lax.psum_scatter(
        lax.dot_general(
            piece, grad_raw, (((0,), (0,)), ((), ())), preferred_element_type=jnp.float32
        ),
        ("section", "chan", "batch"),
        scatter_dimension=0,
        tiled=True,
    )
    return (late_out, grad_late, grad_early)


def solution(mesh):
    return jax.shard_map(
        body,
        mesh=mesh,
        in_specs=(
            P("section", "batch", "chan", None, None),
            P(),
            P(),
            P(),
            P(None, "chan"),
            P("chan"),
            P("chan"),
            P("section", "batch", None, "chan"),
        ),
        out_specs=(
            P("section", "batch", None, "chan"),
            P(None, "chan"),
            P(("section", "chan", "batch"), None),
        ),
        check_vma=False,
    )
```

profile of v0, /device:TPU:0, one launch (start us, length us, event | category | flops | bytes accessed | tf_op | source)
XLA Modules:
  0.0 587.5 jit_solution(7332873103546466312)
XLA Ops:
  7.2 0.0 copy-start
  7.2 0.0 all-gather.3.cloned.1.call-start
  7.2 1.0 copy-done
  8.2 3.5 convert_reduce_fusion
  11.7 63.0 %all-reduce.1 = (f32[2048]{0:T(1024)S(1)}, f32[2048]{0:T(1024)S(1)}) all-reduce(f32[2048]{0:T(1024)S(1)} %get-tuple-element.16, f32[2048]{0:T(1024)S(1)} %get-tuple-element.15), channel_id=1, replica_groups=mesh['section'=2,'chan'=4,'batch'=4] {'chan','batch'}, use_global_device_ids=true, to_apply=%region_3.0 | all-reduce | flops 4096 | bytes 32768 | tf_op jit(solution)/shard_map/psum | solution.py:26
  74.7 1.7 fusion.16
  76.4 0.0 all-gather.3.cloned.1.call-update
  76.4 0.0 copy-start.2
  76.4 0.0 copy-start.4
  76.4 0.0 reduce-scatter.5.cloned.1.call-start
  76.5 78.1 %all-gather.3.cloned.1.call-done = bf16[1024,2048]{1,0:T(8,128)(2,1)} async-done(((bf16[256,2048]{1,0:T(8,128)(2,1)}), bf16[1024,2048]{1,0:T(8,128)(2,1)}) %all-gather.3.cloned.1.call-update) | async-done | bytes 4194320 | tf_op jit(solution)/shard_map/all_gather | solution.py:32
  154.6 14.5 %fusion.38 = (f32[2048]{0:T(1024)S(1)}, f32[2048]{0:T(1024)S(1)}, f32[1024,2048]{1,0:T(8,128)}) fusion(bf16[1024,2048]{1,0:T(8,128)(2,1)} %all-gather.3.cloned.1.call-done, bf16[2048,2048]{1,0:T(8,128)(2,1)} %param.12), kind=kOutput, calls=%fused_computation.56 | convolution fusion | flops 8596221952 | bytes 20987904 | tf_op jit(solution)/shard_map/dot_general | solution.py:34
  169.1 11.2 %all-reduce.3 = (f32[2048]{0:T(1024)S(1)}, f32[2048]{0:T(1024)S(1)}) all-reduce(f32[2048]{0:T(1024)S(1)} %get-tuple-element.12, f32[2048]{0:T(1024)S(1)} %get-tuple-element.11), channel_id=1, replica_groups=mesh['section'=2,'chan'=4,'batch'=4] {'batch'}, use_global_device_ids=true, to_apply=%region_7.0 | all-reduce | flops 4096 | bytes 32768 | tf_op jit(solution)/shard_map/psum | solution.py:36
  180.3 7.6 %fusion.37 = (f32[2048]{0:T(1024)S(1)}, f32[2048]{0:T(1024)S(1)}) fusion(f32[2048]{0:T(1024)S(1)} %copy-done.4, f32[2048]{0:T(1024)S(1)} %copy-done.2, f32[2048]{0:T(1024)S(1)} %get-tuple-element.30, f32[1024,2048]{1,0:T(8,128)} %get-tuple-element.34, f32[2048]{0:T(1024)S(1)} %get-tuple-element.32, bf16[1,4,256,2048]{3,2,1,0:T(8,128)(2,1)} %param.15), kind=kLoop, calls=%fused_computation.55 | loop fusion | flops 33550336 | bytes 12632064 | tf_op jit(solution)/shard_map/reduce_sum | solution.py:43
  187.9 10.3 %all-reduce.2 = (f32[2048]{0:T(1024)S(1)}, f32[2048]{0:T(1024)S(1)}) all-reduce(f32[2048]{0:T(1024)S(1)} %get-tuple-element.10, f32[2048]{0:T(1024)S(1)} %get-tuple-element.9), channel_id=1, replica_groups=mesh['section'=2,'chan'=4,'batch'=4] {'batch'}, use_global_device_ids=true, to_apply=%region_11.0 | all-reduce | flops 4096 | bytes 32768 | tf_op jit(solution)/shard_map/psum | solution.py:43
  198.2 9.6 %multiply_convert_fusion = (bf16[1024,2048]{1,0:T(8,128)(2,1)S(1)}, bf16[1024,2048]{1,0:T(8,128)(2,1)}) fusion(f32[1024,2048]{1,0:T(8,128)} %get-tuple-element.34, f32[2048]{0:T(1024)S(1)} %get-tuple-element.35, f32[2048]{0:T(1024)S(1)} %get-tuple-element.36, f32[2048]{0:T(1024)S(1)} %get-tuple-element.29, f32[2048]{0:T(1024)S(1)} %get-tuple-element.30, ...), kind=kLoop, calls=%fused_computation.3 | loop fusion | flops 41943040 | bytes 21028864 | tf_op jit(solution)/shard_map/convert_element_type | solution.py:46
  207.9 2.0 copy-done.1
  209.8 12.6 %fusion.2 = bf16[4,256,2048]{2,1,0:T(8,128)(2,1)} fusion(bf16[4,256,2048]{2,1,0:T(8,128)(2,1)S(1)} %bitcast.43, bf16[2048,2048]{1,0:T(8,128)(2,1)} %param.12), kind=kOutput, calls=%fused_computation.12 | convolution fusion | flops 8592031744 | bytes 16777216 | tf_op jit(solution)/shard_map/ipl,al->ipa/dot_general | solution.py:54
  222.4 0.0 reduce-scatter.5.cloned.1.call-update
  222.5 0.0 all-reduce.6.cloned.1.call-start
  222.5 14.0 %convolution_convert_fusion = bf16[2048,2048]{1,0:T(8,128)(2,1)} fusion(bf16[1024,2048]{1,0:T(8,128)(2,1)} %all-gather.3.cloned.1.call-done, bf16[1024,2048]{1,0:T(8,128)(2,1)} %copy-done.1), kind=kOutput, calls=%fused_computation.10 | convolution fusion | flops 8594128896 | bytes 16777216 | tf_op jit(solution)/shard_map/dot_general | solution.py:47
  236.5 0.0 all-reduce.6.cloned.1.call-update
  236.6 0.3 reduce-scatter.7.cloned.1.call-start
  236.8 60.1 %reduce-scatter.5.cloned.1.call-done = bf16[1,256,2048]{2,1,0:T(8,128)(2,1)} async-done(((bf16[4,256,2048]{2,1,0:T(8,128)(2,1)}), bf16[1,256,2048]{2,1,0:T(8,128)(2,1)}) %reduce-scatter.5.cloned.1.call-update) | async-done | bytes 1048592 | tf_op jit(solution)/shard_map/reduce_scatter | solution.py:53
  296.9 2.5 fusion.36
  299.5 62.0 %all-reduce = (f32[2048]{0:T(1024)S(1)}, f32[2048]{0:T(1024)S(1)}) all-reduce(f32[2048]{0:T(1024)S(1)} %get-tuple-element.14, f32[2048]{0:T(1024)S(1)} %get-tuple-element.13), channel_id=1, replica_groups=mesh['section'=2,'chan'=4,'batch'=4] {'chan','batch'}, use_global_device_ids=true, to_apply=%region_17.0 | all-reduce | flops 4096 | bytes 32768 | tf_op jit(solution)/shard_map/psum | solution.py:63
  361.5 6.8 %convolution_bitcast_fusion = f32[1024,2048]{0,1:T(8,128)} fusion(bf16[256,2048]{1,0:T(8,128)(2,1)S(1)} %get-tuple-element.33, f32[2048]{0:T(1024)S(1)} %broadcast_multiply_fusion, f32[2048]{0:T(1024)S(1)} %broadcast_multiply_fusion.1, f32[2048]{0:T(1024)S(1)} %get-tuple-element.27, f32[2048]{0:T(1024)S(1)} %get-tuple-element.28, ...), kind=kOutput, calls=%fused_computation.11 | convolution fusion | flops 1083703296 | bytes 11067392 | tf_op jit(solution)/shard_map/dot_general | solution.py:73
  368.2 9.3 %copy.13 = f32[1024,2048]{1,0:T(8,128)} copy(f32[1024,2048]{0,1:T(8,128)} %convolution_bitcast_fusion) | data formatting | bytes 16777216
  377.6 0.0 reduce-scatter.7.cloned.1.call-update
  377.6 51.7 %all-reduce.6.cloned.1.call-done = bf16[2048,2048]{1,0:T(8,128)(2,1)} async-done(((bf16[2048,2048]{1,0:T(8,128)(2,1)}), bf16[2048,2048]{1,0:T(8,128)(2,1)}) %all-reduce.6.cloned.1.call-update) | async-done | bytes 8388624 | tf_op jit(solution)/shard_map/psum | solution.py:50
  429.3 11.7 %convert_element_type.42 = f32[2048,2048]{1,0:T(8,128)} convert(bf16[2048,2048]{1,0:T(8,128)(2,1)} %all-reduce.6.cloned.1.call-done) | non-fusion elementwise | flops 4194304 | bytes 25165824 | tf_op jit(solution)/shard_map/convert_element_type | solution.py:50
  441.0 140.0 %reduce-scatter.7.cloned.1.call-done = f32[32,2048]{1,0:T(8,128)} async-done(((f32[1024,2048]{1,0:T(8,128)}), f32[32,2048]{1,0:T(8,128)}) %reduce-scatter.7.cloned.1.call-update) | async-done | bytes 262160
  (12 shorter events, 0.0 us)
Async XLA Ops:
  7.2 1.0 copy-start
  7.2 67.5 %copy-start.3 = (f32[2048]{0:T(1024)S(1)}, f32[2048]{0:T(1024)}, u32[]{:S(2)}) copy-start(f32[2048]{0:T(1024)} %param.10) | copy-start | bytes 24580
  7.2 67.5 %copy-start.5 = (f32[2048]{0:T(1024)S(1)}, f32[2048]{0:T(1024)}, u32[]{:S(2)}) copy-start(f32[2048]{0:T(1024)} %param.11) | copy-start | bytes 24580
  7.2 147.4 %all-gather.3.cloned.1.call-start = ((), (), s32[]{:S(2)}) async-start(), calls=%async_computation.4 | async-start | bytes 5242880 | tf_op jit(solution)/shard_map/all_gather | solution.py:32
  76.4 103.9 %copy-start.2 = (f32[2048]{0:T(1024)S(1)}, f32[2048]{0:T(1024)}, u32[]{:S(2)}) copy-start(f32[2048]{0:T(1024)} %param.13) | copy-start | bytes 24580
  76.4 103.9 %copy-start.4 = (f32[2048]{0:T(1024)S(1)}, f32[2048]{0:T(1024)}, u32[]{:S(2)}) copy-start(f32[2048]{0:T(1024)} %param.14) | copy-start | bytes 24580
  76.4 220.5 %reduce-scatter.5.cloned.1.call-start = ((), (), s32[]{:S(2)}) async-start(), calls=%async_computation.3 | async-start | bytes 5242880 | tf_op jit(solution)/shard_map/reduce_scatter | solution.py:53
  207.9 2.0 copy-start.1
  222.5 206.9 %all-reduce.6.cloned.1.call-start = ((), (), s32[]{:S(2)}) async-start(), calls=%async_computation.2 | async-start | bytes 16777216 | tf_op jit(solution)/shard_map/psum | solution.py:50
  236.6 344.5 %reduce-scatter.7.cloned.1.call-start = ((), (), s32[]{:S(2)}) async-start(), calls=%async_computation.5 | async-start | bytes 8650752
Sparse Core Ops, SparseCore 0:
  76.5 78.0 all-gather.2
  222.6 74.3 reduce-scatter.4
  301.4 127.8 all-reduce.5
  432.0 148.9 reduce-scatter.6
where the time goes:
time: 588 us
  waiting for transfers between devices  330 us (56%)
  blocking collectives  147 us (25%)
  matrix products  51.3 us (9%)
  other arithmetic  33.1 us (6%)
  between operations  13.8 us (2%)
  local copies, waits for them, and re-layouts  12.3 us (2%)
    unnamed x5, waiting for transfers between devices  140 us
    all_gather x1, waiting for transfers between devices, body(): act_full = lax.all_gather(act_local, 'chan', axis=0, tiled=True)  78.1 us
    psum x1, blocking collectives, body(): lax.psum((jnp.sum(raw_f, 0), jnp.sum(raw_f * raw_f, 0)), ('chan', 'batch'))  63 us
    psum x1, blocking collectives, body(): lax.psum((jnp.sum(grad_pre, 0), jnp.sum(grad_pre * normed_e, 0)), ('chan'...  62 us
    reduce_scatter x1, waiting for transfers between devices, body(): lax.psum_scatter(jnp.einsum('ipl,al->ipa', piece, w_late, preferred_eleme...  60.1 us
    psum x1, waiting for transfers between devices, body(): lax.psum(local_late.astype(jnp.bfloat16), ('section', 'batch'))  51.7 us
    dot_general x1, matrix products, body(): late = jnp.dot(act_rows, w_late, preferred_element_type=jnp.float32)  14.5 us
    dot_general x1, matrix products, body(): lax.dot_general(act_rows, grad_h, (((0,), (0,)), ((), ())), preferred_ele...  14 us
  transfers between devices with their start and end apart: 4, of which 4 were waited for; matrix products, arithmetic and copies ran while one was open for 8% of the time, Pallas kernels for 0%

commit v1 on v0

v1 whole, which is shorter than its diff:
```python
import functools

import jax
import jax.numpy as jnp
from jax import lax
from jax.experimental import pallas as pl
from jax.experimental.pallas import tpu as pltpu
from jax.sharding import PartitionSpec as P

MESH = pl.DeviceIdType.MESH


def smooth_gate(values):
    return values * jax.nn.sigmoid(values)


def smooth_slope(values):
    sig = jax.nn.sigmoid(values)
    return sig * (1.0 + values * (1.0 - sig))


def sums_kernel(n, x_ref, o_ref, buf, send_sem, recv_sem):
    me = lax.axis_index("batch")
    peers = [lax.rem(me + d, n) for d in range(1, n)]
    barrier = pltpu.get_barrier_semaphore()
    for peer in peers:
        pl.semaphore_signal(barrier, inc=1, device_id={"batch": peer}, device_id_type=MESH)
    buf[me] = x_ref[...]
    pl.semaphore_wait(barrier, n - 1)
    copies = []
    for peer in peers:
        copy = pltpu.make_async_remote_copy(
            src_ref=x_ref,
            dst_ref=buf.at[me],
            send_sem=send_sem.at[peer],
            recv_sem=recv_sem.at[me],
            device_id={"batch": peer},
            device_id_type=MESH,
        )
        copy.start()
        copies.append(copy)
    for peer in peers:
        pltpu.make_async_remote_copy(
            src_ref=x_ref,
            dst_ref=buf.at[peer],
            send_sem=send_sem.at[peer],
            recv_sem=recv_sem.at[peer],
            device_id={"batch": peer},
            device_id_type=MESH,
        ).wait_recv()
    total = buf[0]
    for k in range(1, n):
        total = total + buf[k]
    o_ref[...] = total
    for copy in copies:
        copy.wait_send()


def batch_sums(one, two, collective_id):
    n = lax.axis_size("batch")
    width = one.shape[0]
    x = jnp.concatenate([one, two]).reshape(-1, 128)
    out = pl.pallas_call(
        functools.partial(sums_kernel, n),
        out_shape=jax.ShapeDtypeStruct(x.shape, x.dtype),
        in_specs=[pl.BlockSpec(memory_space=pltpu.VMEM)],
        out_specs=pl.BlockSpec(memory_space=pltpu.VMEM),
        scratch_shapes=[
            pltpu.VMEM((n,) + x.shape, x.dtype),
            pltpu.SemaphoreType.DMA((n,)),
            pltpu.SemaphoreType.DMA((n,)),
        ],
        compiler_params=pltpu.CompilerParams(collective_id=collective_id, has_side_effects=True),
        name=f"batch_sums_{collective_id}",
    )(x)
    out = out.reshape(2, width)
    return out[0], out[1]


def body(images, w_early, gain_early, bias_early, w_late, gain_late, bias_late, cotangent):
    width_in = images.shape[-1]
    width_mid = w_early.shape[1]
    width_out = w_late.shape[1]
    batch_count = lax.axis_size("batch")
    own = images.reshape(-1, width_in)
    flat_in = lax.all_gather(own, "chan", axis=0, tiled=True)
    total_rows = flat_in.shape[0] * batch_count

    raw = jnp.dot(flat_in, w_early, preferred_element_type=jnp.float32).astype(jnp.bfloat16)
    raw_f = raw.astype(jnp.float32)
    sum_one, sum_two = batch_sums(jnp.sum(raw_f, 0), jnp.sum(raw_f * raw_f, 0), 0)
    mean_e = sum_one / total_rows
    rstd_e = lax.rsqrt(sum_two / total_rows - mean_e * mean_e + 1e-05)
    normed_e = (raw_f - mean_e) * rstd_e
    pre_e = normed_e * gain_early + bias_early
    act = smooth_gate(pre_e).astype(jnp.bfloat16)

    late = jnp.dot(act, w_late, preferred_element_type=jnp.float32)
    late_one, late_two = batch_sums(jnp.sum(late, 0), jnp.sum(late * late, 0), 1)
    mean_l = late_one / total_rows
    rstd_l = lax.rsqrt(late_two / total_rows - mean_l * mean_l + 1e-05)
    normed_l = (late - mean_l) * rstd_l
    pre_l = normed_l * gain_late + bias_late
    late_out = smooth_gate(pre_l).astype(jnp.bfloat16).reshape(cotangent.shape)
    grad_y = cotangent.reshape(-1, width_out).astype(jnp.float32) * smooth_slope(pre_l)
    back_one, back_two = batch_sums(jnp.sum(grad_y, 0), jnp.sum(grad_y * normed_l, 0), 2)
    grad_h = (
        gain_late * rstd_l * (grad_y - back_one / total_rows - normed_l * (back_two / total_rows))
    ).astype(jnp.bfloat16)

    grad_act = lax.dot_general(
        grad_h, w_late, (((1,), (1,)), ((), ())), preferred_element_type=jnp.float32
    )
    grad_pre = grad_act * smooth_slope(pre_e)
    early_one, early_two = batch_sums(jnp.sum(grad_pre, 0), jnp.sum(grad_pre * normed_e, 0), 3)
    grad_raw = (
        gain_early
        * rstd_e
        * (grad_pre - early_one / total_rows - normed_e * (early_two / total_rows))
    ).astype(jnp.bfloat16)
    part_early = lax.dot_general(
        flat_in, grad_raw, (((0,), (0,)), ((), ())), preferred_element_type=jnp.float32
    ).astype(jnp.bfloat16)
    grad_early = lax.psum_scatter(
        part_early, ("section", "chan", "batch"), scatter_dimension=0, tiled=True
    ).astype(jnp.float32)

    part_late = lax.dot_general(
        act, grad_h, (((0,), (0,)), ((), ())), preferred_element_type=jnp.float32
    ).astype(jnp.bfloat16)
    grad_late = lax.psum(part_late, ("section", "batch")).astype(jnp.float32)
    return (late_out, grad_late, grad_early)


def solution(mesh):
    return jax.shard_map(
        body,
        mesh=mesh,
        in_specs=(
            P("section", "batch", "chan", None, None),
            P(),
            P(),
            P(),
            P(None, "chan"),
            P("chan"),
            P("chan"),
            P("section", "batch", None, "chan"),
        ),
        out_specs=(
            P("section", "batch", None, "chan"),
            P(None, "chan"),
            P(("section", "chan", "batch"), None),
        ),
        check_vma=False,
    )
```

time: 588 us -> 417 us (0.71)
  blocking collectives: 147 us -> 0 us
  waiting for transfers between devices: 330 us -> 266 us
  Pallas kernels: 0 us -> 21 us
  matrix products: 51.3 us -> 69 us
    psum x4 -> x0, blocking collectives: 147 us -> none  [the longest x1 63 us: body(): lax.psum((jnp.sum(raw_f, 0), jnp.sum(raw_f * raw_f, 0)), ('chan', 'batch'))]
    reduce_scatter x1 -> x0, waiting for transfers between devices: 60.1 us -> none  [body(): lax.psum_scatter(jnp.einsum('ipl,al->ipa', piece, w_late, preferred_eleme...]
    psum x1, waiting for transfers between devices: 51.7 us -> 82.1 us  [body(): grad_late = lax.psum(part_late, ('section', 'batch')).astype(jnp.float32)]
    all_gather x1, waiting for transfers between devices: 78.1 us -> 50.3 us  [body(): flat_in = lax.all_gather(own, 'chan', axis=0, tiled=True)]
    pallas_call x0 -> x4, Pallas kernels: none -> 21 us  [batch_sums(): pl.pallas_call(functools.partial(sums_kernel, n), out_shape=jax.ShapeDtyp...]
    dot_general x4, matrix products: 47.9 us -> 59.7 us  [the longest x1 18.5 us: body(): lax.dot_general(grad_h, w_late, (((1,), (1,)), ((), ())), preferred_eleme...]
    unnamed x5 -> x4, waiting for transfers between devices: 140 us -> 133 us
    unnamed x13 -> x17, local copies, waits for them, and re-layouts: 12.3 us -> 10.6 us
  transfers between devices with their start and end apart: 4 -> 3, of which waited for: 4 -> 3; matrix products, arithmetic and copies ran while one was open for 8% -> 12% of each run, Pallas kernels for 0% -> 1%
where the time goes in v1:
time: 417 us; the launch traced here: 416 us
  waiting for transfers between devices  266 us (64%)
  matrix products  69 us (17%)
  other arithmetic  35.7 us (9%)
  Pallas kernels  21 us (5%)
  between operations  13.9 us (3%)
  local copies, waits for them, and re-layouts  10.6 us (3%)
    unnamed x4, waiting for transfers between devices  133 us
    psum x1, waiting for transfers between devices, body(): grad_late = lax.psum(part_late, ('section', 'batch')).astype(jnp.float32)  82.1 us
    all_gather x1, waiting for transfers between devices, body(): flat_in = lax.all_gather(own, 'chan', axis=0, tiled=True)  50.3 us
    pallas_call x4, Pallas kernels, batch_sums(): pl.pallas_call(functools.partial(sums_kernel, n), out_shape=jax.ShapeDtyp...  21 us
    dot_general x1, matrix products, body(): lax.dot_general(grad_h, w_late, (((1,), (1,)), ((), ())), preferred_eleme...  18.5 us
    dot_general x1, matrix products, body(): late = jnp.dot(act, w_late, preferred_element_type=jnp.float32)  16.7 us
    dot_general x1, matrix products, body(): lax.dot_general(act, grad_h, (((0,), (0,)), ((), ())), preferred_element_...  12.7 us
    dot_general x1, matrix products, body(): lax.dot_general(flat_in, grad_raw, (((0,), (0,)), ((), ())), preferred_el...  11.8 us
  transfers between devices with their start and end apart: 3, of which 3 were waited for; matrix products, arithmetic and copies ran while one was open for 12% of the time, Pallas kernels for 1%

profile of v1, /device:TPU:0, one launch (start us, length us, event | category | flops | bytes accessed | tf_op | source)
XLA Modules:
  0.0 415.8 jit_solution(6498136967342366972)
XLA Ops:
  7.2 0.7 all-gather.3.cloned.1.call-update
  7.9 0.0 all-reduce.2.cloned.1.call-start
  8.0 50.3 %all-gather.3.cloned.1.call-done = bf16[1,1,1,1024,1024]{4,3,2,1,0:T(8,128)(2,1)} async-done(((bf16[1,1,1,256,1024]{4,3,2,1,0:T(8,128)(2,1)}), bf16[1,1,1,1024,1024]{4,3,2,1,0:T(8,128)(2,1)}) %all-gather.3.cloned.1.call-update) | async-done | bytes 2097168 | tf_op jit(solution)/shard_map/all_gather | solution.py:86
  58.2 9.3 %convert_reduce_fusion = (f32[2048]{0:T(1024)S(1)}, f32[2048]{0:T(1024)S(1)}, bf16[1024,2048]{1,0:T(8,128)(2,1)}) fusion(bf16[1024,2048]{1,0:T(8,128)(2,1)} %param.9, bf16[1,1,1,1024,1024]{4,3,2,1,0:T(8,128)(2,1)} %all-gather.3.cloned.1.call-done), kind=kOutput, calls=%fused_computation.2 | convolution fusion | flops 4305448960 | bytes 10502144 | tf_op jit(solution)/shard_map/dot_general | solution.py:89
  67.5 0.6 pad_maximum_fusion.x_ref
  68.1 5.1 %batch_sums_0.1 = f32[32,128]{1,0:T(8,128)} custom-call(f32[32,128]{1,0:T(8,128)} %pad_maximum_fusion.x_ref), custom_call_target="tpu_custom_call" | custom-call | tf_op jit(solution)/shard_map/batch_sums_0/pallas_call | solution.py:63
  73.3 0.7 multiply_bitcast_fusion.5
  74.0 0.7 fusion.36
  74.7 16.7 %fusion.42 = (f32[2048]{0:T(1024)S(1)}, f32[2048]{0:T(1024)S(1)}, f32[1024,2048]{1,0:T(8,128)}) fusion(bf16[2048,2048]{1,0:T(8,128)(2,1)} %param.12, bf16[1024,2048]{1,0:T(8,128)(2,1)} %get-tuple-element.27, f32[2048]{0:T(1024)S(1)} %copy-done.5, f32[2048]{0:T(1024)S(1)} %copy-done.3, f32[2048]{0:T(1024)S(1)} %get-tuple-element.20, ...), kind=kOutput, calls=%fused_computation.65 | convolution fusion | flops 8617193472 | bytes 21020672 | tf_op jit(solution)/shard_map/dot_general | solution.py:98
  91.4 0.6 pad_maximum_fusion.1.x_ref
  92.0 5.1 %batch_sums_1.1 = f32[32,128]{1,0:T(8,128)} custom-call(f32[32,128]{1,0:T(8,128)} %pad_maximum_fusion.1.x_ref), custom_call_target="tpu_custom_call" | custom-call | tf_op jit(solution)/shard_map/batch_sums_1/pallas_call | solution.py:63
  97.2 0.7 multiply_bitcast_fusion.4
  97.9 0.7 fusion.33
  98.6 7.5 %fusion.40 = (f32[2048]{0:T(1024)S(1)}, f32[2048]{0:T(1024)S(1)}) fusion(f32[2048]{0:T(1024)S(1)} %copy-done.2, f32[2048]{0:T(1024)S(1)} %copy-done.1, f32[2048]{0:T(1024)S(1)} %get-tuple-element.24, f32[1024,2048]{1,0:T(8,128)} %get-tuple-element.28, f32[2048]{0:T(1024)S(1)} %multiply_bitcast_fusion.4, bf16[1,4,256,2048]{3,2,1,0:T(8,128)(2,1)} %param.15), kind=kLoop, calls=%fused_computation.63 | loop fusion | flops 33550336 | bytes 12632064 | tf_op jit(solution)/shard_map/reduce_sum | solution.py:106
  106.2 0.6 pad_maximum_fusion.2.x_ref
  106.8 5.1 %batch_sums_2.1 = f32[32,128]{1,0:T(8,128)} custom-call(f32[32,128]{1,0:T(8,128)} %pad_maximum_fusion.2.x_ref), custom_call_target="tpu_custom_call" | custom-call | tf_op jit(solution)/shard_map/batch_sums_2/pallas_call | solution.py:63
  111.9 0.7 multiply_bitcast_fusion.3
  112.6 9.8 %multiply_convert_fusion = (bf16[1024,2048]{1,0:T(8,128)(2,1)S(1)}, bf16[1024,2048]{1,0:T(8,128)(2,1)}) fusion(f32[1024,2048]{1,0:T(8,128)} %get-tuple-element.28, f32[2048]{0:T(1024)S(1)} %get-tuple-element.26, f32[2048]{0:T(1024)S(1)} %get-tuple-element.25, f32[2048]{0:T(1024)S(1)} %get-tuple-element.23, f32[2048]{0:T(1024)S(1)} %get-tuple-element.24, ...), kind=kLoop, calls=%fused_computation.24 | loop fusion | flops 41943040 | bytes 21028864 | tf_op jit(solution)/shard_map/convert_element_type | solution.py:109
  122.4 2.0 copy-done
  124.4 12.7 %convolution_convert_fusion = bf16[2048,2048]{1,0:T(8,128)(2,1)} fusion(bf16[1024,2048]{1,0:T(8,128)(2,1)S(1)} %get-tuple-element.17, bf16[1024,2048]{1,0:T(8,128)(2,1)S(1)} %copy-done.6, f32[2048]{0:T(1024)S(1)} %copy-done.5, f32[2048]{0:T(1024)S(1)} %copy-done.3, f32[2048]{0:T(1024)S(1)} %get-tuple-element.20, f32[2048]{0:T(1024)S(1)} %multiply_bitcast_fusion.5), kind=kOutput, calls=%fused_computation.31 | convolution fusion | flops 8615100416 | bytes 16809984 | tf_op jit(solution)/shard_map/dot_general | solution.py:128
  137.1 0.0 reduce-scatter.4.cloned.1.call-start
  137.1 18.5 %fusion.41 = (f32[2048]{0:T(1024)S(1)}, f32[2048]{0:T(1024)S(1)}, f32[1024,2048]{1,0:T(8,128)}) fusion(f32[2048]{0:T(1024)S(1)} %get-tuple-element.20, f32[2048]{0:T(1024)S(1)} %multiply_bitcast_fusion.5, bf16[1024,2048]{1,0:T(8,128)(2,1)} %get-tuple-element.27, f32[2048]{0:T(1024)S(1)} %copy-done.5, f32[2048]{0:T(1024)S(1)} %copy-done.3, ...), kind=kOutput, calls=%fused_computation.64 | convolution fusion | flops 8623484928 | bytes 25214976 | tf_op jit(solution)/shard_map/dot_general | solution.py:111
  155.6 0.6 pad_maximum_fusion.3.x_ref
  156.2 5.6 %batch_sums_3.1 = f32[32,128]{1,0:T(8,128)} custom-call(f32[32,128]{1,0:T(8,128)} %pad_maximum_fusion.3.x_ref), custom_call_target="tpu_custom_call" | custom-call | tf_op jit(solution)/shard_map/batch_sums_3/pallas_call | solution.py:63
  161.9 0.7 multiply_bitcast_fusion.1
  162.6 11.8 %convert_bitcast_fusion = bf16[1024,2048]{0,1:T(8,128)(2,1)} fusion(bf16[1024,2048]{1,0:T(8,128)(2,1)} %get-tuple-element.27, f32[1024,2048]{1,0:T(8,128)} %get-tuple-element.29, f32[2048]{0:T(1024)S(1)} %get-tuple-element.22, f32[2048]{0:T(1024)S(1)} %get-tuple-element.21, f32[2048]{0:T(1024)S(1)} %get-tuple-element.19, f32[2048]{0:T(1024)S(1)} %get-tuple-element.20, ...), kind=kOutput, calls=%fused_computation.33 | convolution fusion | flops 4313841664 | bytes 18915328 | tf_op jit(solution)/shard_map/dot_general | solution.py:121
  174.5 6.5 %copy.13 = bf16[1024,2048]{1,0:T(8,128)(2,1)} copy(bf16[1024,2048]{0,1:T(8,128)(2,1)} %convert_bitcast_fusion) | data formatting | bytes 8388608
  181.0 82.1 %all-reduce.2.cloned.1.call-done = bf16[2048,2048]{1,0:T(8,128)(2,1)} async-done(((bf16[2048,2048]{1,0:T(8,128)(2,1)}), bf16[2048,2048]{1,0:T(8,128)(2,1)}) %all-reduce.2.cloned.1.call-update) | async-done | bytes 8388624 | tf_op jit(solution)/shard_map/psum | solution.py:131
  263.1 11.7 %convert_element_type.47 = f32[2048,2048]{1,0:T(8,128)} convert(bf16[2048,2048]{1,0:T(8,128)(2,1)} %all-reduce.2.cloned.1.call-done) | non-fusion elementwise | flops 4194304 | bytes 25165824 | tf_op jit(solution)/shard_map/convert_element_type | solution.py:131
  274.8 132.4 %reduce-scatter.4.cloned.1.call-done = bf16[32,2048]{1,0:T(8,128)(2,1)} async-done(((bf16[1024,2048]{1,0:T(8,128)(2,1)}), bf16[32,2048]{1,0:T(8,128)(2,1)}) %reduce-scatter.4.cloned.1.call-update) | async-done | bytes 131088
  407.2 1.2 copy.14
  408.4 0.9 copy.12
  (16 shorter events, 0.1 us)
Async XLA Ops:
  7.2 51.1 %all-gather.3.cloned.1.call-start = ((), (), s32[]{:S(2)}) async-start(), calls=%async_computation.2 | async-start | bytes 2621440 | tf_op jit(solution)/shard_map/all_gather | solution.py:86
  7.9 66.1 %copy-start.3 = (f32[2048]{0:T(1024)S(1)}, f32[2048]{0:T(1024)}, u32[]{:S(2)}) copy-start(f32[2048]{0:T(1024)} %param.10) | copy-start | bytes 24580
  7.9 66.8 %copy-start.5 = (f32[2048]{0:T(1024)S(1)}, f32[2048]{0:T(1024)}, u32[]{:S(2)}) copy-start(f32[2048]{0:T(1024)} %param.11) | copy-start | bytes 24580
  7.9 255.2 %all-reduce.2.cloned.1.call-start = ((), (), s32[]{:S(2)}) async-start(), calls=%async_computation.1 | async-start | bytes 16777216 | tf_op jit(solution)/shard_map/psum | solution.py:131
  74.7 23.2 %copy-start.1 = (f32[2048]{0:T(1024)S(1)}, f32[2048]{0:T(1024)}, u32[]{:S(2)}) copy-start(f32[2048]{0:T(1024)} %param.13) | copy-start | bytes 24580
  74.7 23.9 %copy-start.2 = (f32[2048]{0:T(1024)S(1)}, f32[2048]{0:T(1024)}, u32[]{:S(2)}) copy-start(f32[2048]{0:T(1024)} %param.14) | copy-start | bytes 24580
  112.6 11.8 %copy-start.6 = (bf16[1024,2048]{1,0:T(8,128)(2,1)S(1)}, bf16[1024,2048]{1,0:T(8,128)(2,1)}, u32[]{:S(2)}) copy-start(bf16[1024,2048]{1,0:T(8,128)(2,1)} %get-tuple-element.27) | copy-start | bytes 12582916
  122.4 2.0 copy-start
  137.1 25.5 %copy-start.4 = (bf16[1,1,1,1024,1024]{4,3,2,1,0:T(8,128)(2,1)S(1)}, bf16[1,1,1,1024,1024]{4,3,2,1,0:T(8,128)(2,1)}, u32[]{:S(2)}) copy-start(bf16[1,1,1,1024,1024]{4,3,2,1,0:T(8,128)(2,1)} %all-gather.3.cloned.1.call-done) | copy-start | bytes 6291460
  137.1 270.1 %reduce-scatter.4.cloned.1.call-start = ((), (), s32[]{:S(2)}) async-start(), calls=%async_computation.3 | async-start | bytes 4325376
Sparse Core Ops, SparseCore 0:
  9.6 48.6 all-gather.2
  137.2 125.8 all-reduce.1
  265.5 141.6 reduce-scatter.3

commit v2 on v1

--- a/solution.py
+++ b/solution.py
@@ -77,18 +77,294 @@
     return out[0], out[1]
 
 
+def meet(groups):
+    barrier = pltpu.get_barrier_semaphore()
+    for device in groups:
+        pl.semaphore_signal(barrier, inc=1, device_id=device, device_id_type=MESH)
+    pl.semaphore_wait(barrier, len(groups))
+
+
+def remote(src, dst, send_sem, recv_sem, device):
+    return pltpu.make_async_remote_copy(
+        src_ref=src,
+        dst_ref=dst,
+        send_sem=send_sem,
+        recv_sem=recv_sem,
+        device_id=device,
+        device_id_type=MESH,
+    )
+
+
+def others(axis, n):
+    me = lax.axis_index(axis)
+    return [lax.rem(me + d, n) for d in range(1, n)]
+
+
+def exchange(n, buf, send_sem, recv_sem):
+    me = lax.axis_index("batch")
+    peers = others("batch", n)
+    for peer in peers:
+        remote(buf.at[me], buf.at[me], send_sem.at[peer], recv_sem.at[me], {"batch": peer}).start()
+    for peer in peers:
+        remote(
+            buf.at[peer], buf.at[peer], send_sem.at[peer], recv_sem.at[peer], {"batch": peer}
+        ).wait()
+    total = buf[0]
+    for k in range(1, n):
+        total = total + buf[k]
+    return total
+
+
+def early_kernel(n_chan, n_batch, x_ref, w_ref, x_out, raw_out, sum_out, held, buf,
+                 up_send, up_recv, down_send, down_recv, sum_send, sum_recv):
+    z = lax.axis_index("chan")
+    me = lax.axis_index("batch")
+    rows = x_ref.shape[0]
+    meet([{"chan": p} for p in others("chan", n_chan)]
+         + [{"batch": p} for p in others("batch", n_batch)])
+    held[z] = x_ref[...]
+
+    def up(block):
+        return remote(held.at[block], held.at[block], up_send.at[block], up_recv.at[block],
+                      {"chan": lax.rem(z + 1, n_chan)})
+
+    def down(block):
+        return remote(held.at[block], held.at[block], down_send.at[block], down_recv.at[block],
+                      {"chan": lax.rem(z + n_chan - 1, n_chan)})
+
+    @pl.when(z < n_chan - 1)
+    def _():
+        up(z).start()
+
+    @pl.when(z > 0)
+    def _():
+        down(z).start()
+
+    def multiply(block):
+        at = pl.ds(pl.multiple_of(block * rows, rows), rows)
+        width = w_ref.shape[1]
+        step = min(width, 512)
+
+        @pl.loop(0, width // step)
+        def _(i):
+            cols = pl.ds(pl.multiple_of(i * step, step), step)
+            raw = jnp.dot(
+                held[block], w_ref[:, cols], preferred_element_type=jnp.float32
+            ).astype(jnp.bfloat16)
+            raw_out[at, cols] = raw
+            raw = raw.astype(jnp.float32)
+            buf[me, 0:1, cols] += jnp.sum(raw, 0, keepdims=True)
+            buf[me, 1:2, cols] += jnp.sum(raw * raw, 0, keepdims=True)
+
+    buf[me] = jnp.zeros(buf.shape[1:], buf.dtype)
+    multiply(z)
+    for i in range(1, n_chan):
+        below, above = z - i, z + i
+
+        @pl.when(below >= 0)
+        def _():
+            up(below).wait_recv()
+
+            @pl.when(z < n_chan - 1)
+            def _():
+                up(below).start()
+
+        @pl.when(above < n_chan)
+        def _():
+            down(above).wait_recv()
+
+            @pl.when(z > 0)
+            def _():
+                down(above).start()
+
+        @pl.when(below >= 0)
+        def _():
+            multiply(below)
+
+        @pl.when(above < n_chan)
+        def _():
+            multiply(above)
+
+    sum_out[...] = exchange(n_batch, buf, sum_send, sum_recv)
+    x_out[...] = held[...].reshape(x_out.shape)
+    for block in range(n_chan):
+        @pl.when(jnp.logical_and(block <= z, z < n_chan - 1))
+        def _():
+            up(block).wait_send()
+
+        @pl.when(jnp.logical_and(block >= z, z > 0))
+        def _():
+            down(block).wait_send()
+
+
+def early_forward(x, w, collective_id):
+    n_chan, n_batch = lax.axis_size("chan"), lax.axis_size("batch")
+    rows, width_in = x.shape
+    width = w.shape[1]
+    return pl.pallas_call(
+        functools.partial(early_kernel, n_chan, n_batch),
+        out_shape=(
+            jax.ShapeDtypeStruct((n_chan * rows, width_in), x.dtype),
+            jax.ShapeDtypeStruct((n_chan * rows, width), x.dtype),
+            jax.ShapeDtypeStruct((8, width), jnp.float32),
+        ),
+        in_specs=[pl.BlockSpec(memory_space=pltpu.VMEM)] * 2,
+        out_specs=[pl.BlockSpec(memory_space=pltpu.VMEM)] * 3,
+        scratch_shapes=[
+            pltpu.VMEM((n_chan, rows, width_in), x.dtype),
+            pltpu.VMEM((n_batch, 8, width), jnp.float32),
+        ]
+        + [pltpu.SemaphoreType.DMA((n_chan,))] * 4
+        + [pltpu.SemaphoreType.DMA((n_batch,))] * 2,
+        compiler_params=pltpu.CompilerParams(
+            collective_id=collective_id, has_side_effects=True, vmem_limit_bytes=56 * 2**20
+        ),
+        name="early_forward",
+    )(x, w)
+
+
+def early_grad_kernel(n_sec, n_chan, n_batch, x_ref, g_ref, o_ref, part, pair, mine, low, high, last,
+                      pair_send, pair_recv, low_send, low_recv, high_send, high_recv,
+                      last_send, last_recv):
+    s, z, b = lax.axis_index("section"), lax.axis_index("chan"), lax.axis_index("batch")
+    n_y = n_batch // 2
+    y, core = b // 2, lax.rem(b, 2)
+    sibling = {"batch": y * 2 + 1 - core}
+    plane = [
+        (lax.rem(s + i, n_sec), lax.rem(y + j, n_y))
+        for i in range(n_sec) for j in range(n_y) if i + j > 0
+    ]
+    meet([sibling] + [{"chan": p} for p in others("chan", n_chan)]
+         + [{"section": p, "batch": q * 2 + core} for p, q in plane])
+    rows, width = o_ref.shape
+    span = rows * n_batch
+    step = min(width, 512)
+
+    order = []
+    for i in range(n_chan // 2):
+        order += [i, n_chan - 1 - i]
+    for d in order:
+        lhs = jnp.concatenate(
+            [x_ref[:, (k * n_chan + d) * span:(k * n_chan + d + 1) * span] for k in range(n_sec)], 1
+        ).T
+
+        @pl.loop(0, width // step)
+        def _(i):
+            cols = pl.ds(pl.multiple_of(i * step, step), step)
+            block = jnp.dot(lhs, g_ref[:, cols], preferred_element_type=jnp.float32)
+            part[d, :, :, :, :, cols] = block.reshape(n_sec, n_y, 2, rows, step).astype(jnp.bfloat16)
+
+        remote(part.at[d, :, :, 1 - core], pair.at[d], pair_send.at[d], pair_recv.at[d],
+               sibling).start()
+
+    def from_pair(d):
+        remote(part.at[d, :, :, 1 - core], pair.at[d], pair_send.at[d], pair_recv.at[d],
+               sibling).wait_recv()
+        mine[d] = (
+            part[d, :, :, core].astype(jnp.float32) + pair[d].astype(jnp.float32)
+        ).astype(jnp.bfloat16)
+
+    def lower(d):
+        return remote(mine.at[d], low.at[d], low_send.at[d], low_recv.at[d],
+                      {"chan": lax.rem(z + n_chan - 1, n_chan)})
+
+    def upper(d):
+        return remote(mine.at[d], high.at[d], high_send.at[d], high_recv.at[d],
+                      {"chan": lax.rem(z + 1, n_chan)})
+
+    def add(d, arrived):
+        mine[d] = (mine[d].astype(jnp.float32) + arrived[d].astype(jnp.float32)).astype(jnp.bfloat16)
+
+    for d in order:
+        from_pair(d)
+
+        @pl.when(jnp.logical_and(z == n_chan - 1, d < z))
+        def _():
+            lower(d).start()
+
+        @pl.when(jnp.logical_and(z == 0, d > z))
+        def _():
+            upper(d).start()
+
+    for i in range(n_chan):
+        d, e = i, n_chan - 1 - i
+
+        @pl.when(jnp.logical_and(z < n_chan - 1, d <= z))
+        def _():
+            lower(d).wait_recv()
+            add(d, low)
+
+            @pl.when(d < z)
+            def _():
+                lower(d).start()
+
+        @pl.when(jnp.logical_and(z > 0, e >= z))
+        def _():
+            upper(e).wait_recv()
+            add(e, high)
+
+            @pl.when(e > z)
+            def _():
+                upper(e).start()
+
+    slot = s * n_y + y
+    for p, q in plane:
+        remote(mine.at[z, p, q], last.at[slot], last_send.at[p * n_y + q], last_recv.at[slot],
+               {"section": p, "batch": q * 2 + core}).start()
+    total = mine[z, s, y].astype(jnp.float32)
+    for p, q in plane:
+        there = p * n_y + q
+        remote(mine.at[z, p, q], last.at[there], last_send.at[there], last_recv.at[there],
+               {"section": p, "batch": q * 2 + core}).wait()
+        total = total + last[there].astype(jnp.float32)
+    o_ref[...] = total
+    for d in range(n_chan):
+        remote(part.at[d, :, :, 1 - core], pair.at[d], pair_send.at[d], pair_recv.at[d],
+               sibling).wait_send()
+
+        @pl.when(d < z)
+        def _():
+            lower(d).wait_send()
+
+        @pl.when(d > z)
+        def _():
+            upper(d).wait_send()
+
+
+def early_gradient(x, g, collective_id):
+    n_sec, n_chan, n_batch = (lax.axis_size(a) for a in ("section", "chan", "batch"))
+    n_y = n_batch // 2
+    width = g.shape[1]
+    rows = x.shape[1] // (n_sec * n_chan * n_batch)
+    quarter = (n_chan, n_sec, n_y, rows, width)
+    return pl.pallas_call(
+        functools.partial(early_grad_kernel, n_sec, n_chan, n_batch),
+        out_shape=jax.ShapeDtypeStruct((rows, width), jnp.float32),
+        in_specs=[pl.BlockSpec(memory_space=pltpu.VMEM)] * 2,
+        out_specs=pl.BlockSpec(memory_space=pltpu.VMEM),
+        scratch_shapes=[pltpu.VMEM((n_chan, n_sec, n_y, 2, rows, width), jnp.bfloat16)]
+        + [pltpu.VMEM(quarter, jnp.bfloat16)] * 4
+        + [pltpu.VMEM((n_sec * n_y, rows, width), jnp.bfloat16)]
+        + [pltpu.SemaphoreType.DMA((n_chan,))] * 6
+        + [pltpu.SemaphoreType.DMA((n_sec * n_y,))] * 2,
+        compiler_params=pltpu.CompilerParams(
+            collective_id=collective_id, has_side_effects=True, vmem_limit_bytes=56 * 2**20
+        ),
+        name="early_gradient",
+    )(x, g)
+
+
 def body(images, w_early, gain_early, bias_early, w_late, gain_late, bias_late, cotangent):
     width_in = images.shape[-1]
     width_mid = w_early.shape[1]
     width_out = w_late.shape[1]
     batch_count = lax.axis_size("batch")
     own = images.reshape(-1, width_in)
-    flat_in = lax.all_gather(own, "chan", axis=0, tiled=True)
+    flat_in, raw, sums_e = early_forward(own, w_early, 0)
     total_rows = flat_in.shape[0] * batch_count
 
-    raw = jnp.dot(flat_in, w_early, preferred_element_type=jnp.float32).astype(jnp.bfloat16)
     raw_f = raw.astype(jnp.float32)
-    sum_one, sum_two = batch_sums(jnp.sum(raw_f, 0), jnp.sum(raw_f * raw_f, 0), 0)
+    sum_one, sum_two = sums_e[0], sums_e[1]
     mean_e = sum_one / total_rows
     rstd_e = lax.rsqrt(sum_two / total_rows - mean_e * mean_e + 1e-05)
     normed_e = (raw_f - mean_e) * rstd_e
@@ -108,6 +384,12 @@
         gain_late * rstd_l * (grad_y - back_one / total_rows - normed_l * (back_two / total_rows))
     ).astype(jnp.bfloat16)
 
+    part_late = lax.dot_general(
+        act, grad_h, (((0,), (0,)), ((), ())), preferred_element_type=jnp.float32
+    ).astype(jnp.bfloat16)
+    part_late, grad_h = lax.optimization_barrier((part_late, grad_h))
+    grad_late = lax.psum(part_late, ("section", "batch")).astype(jnp.float32)
+
     grad_act = lax.dot_general(
         grad_h, w_late, (((1,), (1,)), ((), ())), preferred_element_type=jnp.float32
     )
@@ -118,17 +400,7 @@
         * rstd_e
         * (grad_pre - early_one / total_rows - normed_e * (early_two / total_rows))
     ).astype(jnp.bfloat16)
-    part_early = lax.dot_general(
-        flat_in, grad_raw, (((0,), (0,)), ((), ())), preferred_element_type=jnp.float32
-    ).astype(jnp.bfloat16)
-    grad_early = lax.psum_scatter(
-        part_early, ("section", "chan", "batch"), scatter_dimension=0, tiled=True
-    ).astype(jnp.float32)
-
-    part_late = lax.dot_general(
-        act, grad_h, (((0,), (0,)), ((), ())), preferred_element_type=jnp.float32
-    ).astype(jnp.bfloat16)
-    grad_late = lax.psum(part_late, ("section", "batch")).astype(jnp.float32)
+    grad_early = early_gradient(flat_in, grad_raw, 4)
     return (late_out, grad_late, grad_early)
 
 

time: 417 us -> 274 us (0.66)
  the two profiles are of different devices: /device:TPU:0 before, /device:TPU:19 now
where the time goes in v2:
time: 274 us; the launch traced here: 273 us
  Pallas kernels  153 us (56%)
  matrix products  47.8 us (17%)
  other arithmetic  42.2 us (15%)
  between operations  14.1 us (5%)
  waiting for transfers between devices  12.4 us (5%)
    pallas_call x1, Pallas kernels, early_gradient(): pl.pallas_call(functools.partial(early_grad_kernel, n_sec, n_chan, n_batc...  93.9 us
    pallas_call x1, Pallas kernels, early_forward(): pl.pallas_call(functools.partial(early_kernel, n_chan, n_batch), out_shap...  40.4 us
    pallas_call x3, Pallas kernels, batch_sums(): pl.pallas_call(functools.partial(sums_kernel, n), out_shape=jax.ShapeDtyp...  19.1 us
    dot_general x1, matrix products, body(): lax.dot_general(grad_h, w_late, (((1,), (1,)), ((), ())), preferred_eleme...  18.3 us
    dot_general x1, matrix products, body(): late = jnp.dot(act, w_late, preferred_element_type=jnp.float32)  16.5 us
    dot_general x1, matrix products, body(): lax.dot_general(act, grad_h, (((0,), (0,)), ((), ())), preferred_element_...  12.9 us
    psum x1, waiting for transfers between devices, body(): grad_late = lax.psum(part_late, ('section', 'batch')).astype(jnp.float32)  12.3 us
    convert_element_type x1, other arithmetic, body(): grad_late = lax.psum(part_late, ('section', 'batch')).astype(jnp.float32)  11.7 us
  transfers between devices with their start and end apart: 1, of which 1 were waited for; matrix products, arithmetic and copies ran while one was open for 10% of the time, Pallas kernels for 37%

profile of v2, /device:TPU:19, one launch (start us, length us, event | category | flops | bytes accessed | tf_op | source)
XLA Modules:
  0.0 272.5 jit_solution(17502174345281021019)
XLA Ops:
  7.2 0.0 all-reduce.2.cloned.1.call-start
  7.2 40.4 %early_forward.1 = (bf16[1024,1024]{1,0:T(8,128)(2,1)}, bf16[1024,2048]{1,0:T(8,128)(2,1)}, f32[8,2048]{1,0:T(8,128)}) custom-call(bf16[256,1024]{1,0:T(8,128)(2,1)} %bitcast.46, bf16[1024,2048]{1,0:T(8,128)(2,1)} %w_ref.1), custom_call_target="tpu_custom_call" | custom-call | tf_op jit(solution)/shard_map/early_forward/pallas_call | solution.py:204
  47.6 0.9 slice_multiply_fusion.1
  48.5 0.0 copy-start.3
  48.6 0.0 copy-start.4
  48.6 16.5 %fusion.6 = (f32[2048]{0:T(1024)S(1)}, f32[2048]{0:T(1024)S(1)}, f32[1024,2048]{1,0:T(8,128)}) fusion(bf16[2048,2048]{1,0:T(8,128)(2,1)} %param.12, bf16[1024,2048]{1,0:T(8,128)(2,1)} %get-tuple-element.8, f32[2048]{0:T(1024)} %param.11, f32[2048]{0:T(1024)} %param.10, f32[2048]{0:T(1024)S(1)} %bitcast.47, f32[2048]{0:T(1024)S(1)} %bitcast.52), kind=kOutput, calls=%fused_computation.34 | convolution fusion | flops 8617193472 | bytes 21020672 | tf_op jit(solution)/shard_map/dot_general | solution.py:374
  65.1 0.6 pad_maximum_fusion.x_ref
  65.7 7.6 %batch_sums_1.1 = f32[32,128]{1,0:T(8,128)} custom-call(f32[32,128]{1,0:T(8,128)} %pad_maximum_fusion.x_ref), custom_call_target="tpu_custom_call" | custom-call | tf_op jit(solution)/shard_map/batch_sums_1/pallas_call | solution.py:63
  73.3 0.7 multiply_bitcast_fusion.4
  74.0 0.0 copy-done.3
  74.0 0.7 fusion.2
  74.7 0.0 copy-done.4
  74.7 7.5 %fusion.4 = (f32[2048]{0:T(1024)S(1)}, f32[2048]{0:T(1024)S(1)}) fusion(f32[2048]{0:T(1024)S(1)} %copy-done.4, f32[2048]{0:T(1024)S(1)} %copy-done.3, f32[2048]{0:T(1024)S(1)} %get-tuple-element.26, f32[1024,2048]{1,0:T(8,128)} %get-tuple-element.29, f32[2048]{0:T(1024)S(1)} %multiply_bitcast_fusion.4, bf16[1,4,256,2048]{3,2,1,0:T(8,128)(2,1)} %param.15), kind=kLoop, calls=%fused_computation.32 | loop fusion | flops 33550336 | bytes 12632064 | tf_op jit(solution)/shard_map/reduce_sum | solution.py:382
  82.3 0.6 pad_maximum_fusion.1.x_ref
  82.9 5.1 %batch_sums_2.1 = f32[32,128]{1,0:T(8,128)} custom-call(f32[32,128]{1,0:T(8,128)} %pad_maximum_fusion.1.x_ref), custom_call_target="tpu_custom_call" | custom-call | tf_op jit(solution)/shard_map/batch_sums_2/pallas_call | solution.py:63
  88.0 0.7 multiply_bitcast_fusion.3
  88.8 9.8 %multiply_convert_fusion.1 = (bf16[1024,2048]{1,0:T(8,128)(2,1)S(1)}, bf16[1024,2048]{1,0:T(8,128)(2,1)}) fusion(f32[1024,2048]{1,0:T(8,128)} %get-tuple-element.29, f32[2048]{0:T(1024)S(1)} %get-tuple-element.28, f32[2048]{0:T(1024)S(1)} %get-tuple-element.27, f32[2048]{0:T(1024)S(1)} %get-tuple-element.25, f32[2048]{0:T(1024)S(1)} %get-tuple-element.26, ...), kind=kLoop, calls=%fused_computation.4 | loop fusion | flops 41943040 | bytes 21028864 | tf_op jit(solution)/shard_map/convert_element_type | solution.py:385
  98.6 2.0 copy-done.1
  100.5 0.0 copy-done
  100.5 0.0 copy-done.5
  100.5 0.0 copy-done.6
  100.5 12.9 %convolution_convert_fusion = bf16[2048,2048]{1,0:T(8,128)(2,1)} fusion(bf16[1024,2048]{1,0:T(8,128)(2,1)S(1)} %get-tuple-element.12, bf16[1024,2048]{1,0:T(8,128)(2,1)S(1)} %copy-done, f32[2048]{0:T(1024)S(1)} %copy-done.6, f32[2048]{0:T(1024)S(1)} %copy-done.5, f32[2048]{0:T(1024)S(1)} %bitcast.48, f32[2048]{0:T(1024)S(1)} %bitcast.53), kind=kOutput, calls=%fused_computation.15 | convolution fusion | flops 8615100416 | bytes 16809984 | tf_op jit(solution)/shard_map/dot_general | solution.py:387
  113.4 0.0 all-reduce.2.cloned.1.call-update
  113.5 18.3 %fusion.5 = (f32[2048]{0:T(1024)S(1)}, f32[2048]{0:T(1024)S(1)}, f32[1024,2048]{1,0:T(8,128)}) fusion(f32[2048]{0:T(1024)S(1)} %bitcast.50, f32[2048]{0:T(1024)S(1)} %bitcast.54, bf16[1024,2048]{1,0:T(8,128)(2,1)} %get-tuple-element.8, f32[2048]{0:T(1024)S(1)} %copy-done.6, f32[2048]{0:T(1024)S(1)} %copy-done.5, bf16[1024,2048]{1,0:T(8,128)(2,1)} %copy-done.1, ...), kind=kOutput, calls=%fused_computation.33 | convolution fusion | flops 8623484928 | bytes 25214976 | tf_op jit(solution)/shard_map/dot_general | solution.py:393
  131.8 0.6 pad_maximum_fusion.2.x_ref
  132.4 6.3 %batch_sums_3.1 = f32[32,128]{1,0:T(8,128)} custom-call(f32[32,128]{1,0:T(8,128)} %pad_maximum_fusion.2.x_ref), custom_call_target="tpu_custom_call" | custom-call | tf_op jit(solution)/shard_map/batch_sums_3/pallas_call | solution.py:63
  138.8 0.7 multiply_bitcast_fusion.1
  139.5 7.5 %multiply_convert_fusion.g_ref = bf16[1024,2048]{1,0:T(8,128)(2,1)} fusion(f32[1024,2048]{1,0:T(8,128)} %get-tuple-element.30, bf16[1024,2048]{1,0:T(8,128)(2,1)} %get-tuple-element.8, f32[2048]{0:T(1024)S(1)} %get-tuple-element.24, f32[2048]{0:T(1024)S(1)} %get-tuple-element.23, f32[2048]{0:T(1024)S(1)} %mul.140, f32[2048]{0:T(1024)S(1)} %bitcast.51, ...), kind=kLoop, calls=%fused_computation.1 | loop fusion | flops 16777216 | bytes 16818176 | tf_op jit(solution)/shard_map/convert_element_type | solution.py:402
  147.0 93.9 %early_gradient.1 = f32[32,2048]{1,0:T(8,128)} custom-call(bf16[1024,1024]{1,0:T(8,128)(2,1)} %get-tuple-element.11.x_ref, bf16[1024,2048]{1,0:T(8,128)(2,1)} %multiply_convert_fusion.g_ref), custom_call_target="tpu_custom_call" | custom-call | tf_op jit(solution)/shard_map/early_gradient/pallas_call | solution.py:340
  241.0 12.3 %all-reduce.2.cloned.1.call-done = bf16[2048,2048]{1,0:T(8,128)(2,1)} async-done(((bf16[2048,2048]{1,0:T(8,128)(2,1)}), bf16[2048,2048]{1,0:T(8,128)(2,1)}) %all-reduce.2.cloned.1.call-update) | async-done | bytes 8388624 | tf_op jit(solution)/shard_map/psum | solution.py:391
  253.3 11.7 %convert_element_type.34 = f32[2048,2048]{1,0:T(8,128)} convert(bf16[2048,2048]{1,0:T(8,128)(2,1)} %all-reduce.2.cloned.1.call-done) | non-fusion elementwise | flops 4194304 | bytes 25165824 | tf_op jit(solution)/shard_map/convert_element_type | solution.py:391
  265.0 0.7 copy.13
  (7 shorter events, 0.0 us)
Async XLA Ops:
  7.2 246.1 %all-reduce.2.cloned.1.call-start = ((), (), s32[]{:S(2)}) async-start(), calls=%async_computation | async-start | bytes 16777216 | tf_op jit(solution)/shard_map/psum | solution.py:391
  48.5 25.5 %copy-start.3 = (f32[2048]{0:T(1024)S(1)}, f32[2048]{0:T(1024)}, u32[]{:S(2)}) copy-start(f32[2048]{0:T(1024)} %param.13) | copy-start | bytes 24580
  48.6 26.2 %copy-start.4 = (f32[2048]{0:T(1024)S(1)}, f32[2048]{0:T(1024)}, u32[]{:S(2)}) copy-start(f32[2048]{0:T(1024)} %param.14) | copy-start | bytes 24580
  88.8 11.8 %copy-start = (bf16[1024,2048]{1,0:T(8,128)(2,1)S(1)}, bf16[1024,2048]{1,0:T(8,128)(2,1)}, u32[]{:S(2)}) copy-start(bf16[1024,2048]{1,0:T(8,128)(2,1)} %get-tuple-element.8) | copy-start | bytes 12582916
  88.8 11.8 %copy-start.5 = (f32[2048]{0:T(1024)S(1)}, f32[2048]{0:T(1024)}, u32[]{:S(2)}) copy-start(f32[2048]{0:T(1024)} %param.10) | copy-start | bytes 24580
  88.8 11.8 %copy-start.6 = (f32[2048]{0:T(1024)S(1)}, f32[2048]{0:T(1024)}, u32[]{:S(2)}) copy-start(f32[2048]{0:T(1024)} %param.11) | copy-start | bytes 24580
  98.6 2.0 copy-start.1
  241.0 24.0 %copy-start.2 = (f32[32,2048]{1,0:T(8,128)S(1)}, f32[32,2048]{1,0:T(8,128)}, u32[]{:S(2)}) copy-start(f32[32,2048]{1,0:T(8,128)} %early_gradient.1) | copy-start | bytes 786436
Sparse Core Ops, SparseCore 0:
  113.6 139.6 all-reduce.1

commit v3 on v2

--- a/solution.py
+++ b/solution.py
@@ -223,9 +223,16 @@
     )(x, w)
 
 
-def early_grad_kernel(n_sec, n_chan, n_batch, x_ref, g_ref, o_ref, part, pair, mine, low, high, last,
-                      pair_send, pair_recv, low_send, low_recv, high_send, high_recv,
-                      last_send, last_recv):
+CHUNKS = 4
+
+
+def backward_kernel(n_sec, n_chan, n_batch, act_ref, gh_ref, vec_ref, w_hbm, raw_hbm, x_hbm,
+                    late_ref, early_ref, w_ref, raw_ref, x_ref, give, held, gact, buf,
+                    fa, fb, sa, sb, part, pair, mine, low, high, last,
+                    load_sem, put_sem, p1s, p1r, fas, far, fbs, fbr, sas, sar, sbs, sbr,
+                    cas, car, cbs, cbr, p5s, p5r, sum_send, sum_recv,
+                    pair_send, pair_recv, low_send, low_recv, high_send, high_recv,
+                    last_send, last_recv):
     s, z, b = lax.axis_index("section"), lax.axis_index("chan"), lax.axis_index("batch")
     n_y = n_batch // 2
     y, core = b // 2, lax.rem(b, 2)
@@ -234,35 +241,222 @@
         (lax.rem(s + i, n_sec), lax.rem(y + j, n_y))
         for i in range(n_sec) for j in range(n_y) if i + j > 0
     ]
-    meet([sibling] + [{"chan": p} for p in others("chan", n_chan)]
-         + [{"section": p, "batch": q * 2 + core} for p, q in plane])
-    rows, width = o_ref.shape
+    inner = [
+        (lax.rem(s + i, n_sec), lax.rem(y + j, n_y))
+        for i in range(1, n_sec) for j in range(1, n_y)
+    ]
+    loads = [
+        pltpu.make_async_copy(w_hbm, w_ref, load_sem.at[0]),
+        pltpu.make_async_copy(raw_hbm, raw_ref, load_sem.at[1]),
+        pltpu.make_async_copy(x_hbm, x_ref, load_sem.at[2]),
+    ]
+    for load in loads:
+        load.start()
+    meet([{"batch": p} for p in others("batch", n_batch)]
+         + [{"chan": p} for p in others("chan", n_chan)]
+         + [{"section": p} for p in others("section", n_sec)]
+         + [{"section": p, "batch": q * 2 + core} for p, q in inner])
+
+    f32, bf16 = jnp.float32, jnp.bfloat16
+    images, mid = act_ref.shape
+    wide = gh_ref.shape[1]
+    chunk = mid // CHUNKS
+    half, tall = chunk // 2, chunk // 4
+    step = min(wide, 512)
+
+    def dev_sec(p):
+        return {"section": p}
+
+    def dev_y(q):
+        return {"batch": q * 2 + core}
+
+    kinds = [
+        (n_sec, s, dev_sec, n_y, y, dev_y, fa, sa, fas, far, sas, sar, cas, car),
+        (n_y, y, dev_y, n_sec, s, dev_sec, fb, sb, fbs, fbr, sbs, sbr, cbs, cbr),
+    ]
+
+    def span_of(k, t, p):
+        sub = tall // kinds[t][0]
+        return pl.ds(pl.multiple_of(k * chunk + core * half + t * tall + p * sub, sub), sub)
+
+    def to_pair(k):
+        return remote(give.at[k], held.at[k], p1s.at[k], p1r.at[k], sibling)
+
+    def first(k, t, p, slot):
+        n1, me, dev, _, _, _, buf1, _, ss, rs = kinds[t][:10]
+        sub = tall // n1
+        return remote(held.at[k, pl.ds(pl.multiple_of(t * tall + p * sub, sub), sub)],
+                      buf1.at[k, slot], ss.at[k * n1 + p], rs.at[k * n1 + slot], dev(p))
+
+    def second(k, t, q, slot):
+        _, _, _, n2, me, dev, _, buf2, _, _, ss, rs = kinds[t][:12]
+        return remote(buf2.at[k, me], buf2.at[k, slot], ss.at[k * n2 + q], rs.at[k * n2 + slot], dev(q))
+
+    def third(k, t, p, slot):
+        n1, me, dev, _, _, _, buf1 = kinds[t][:7]
+        ss, rs = kinds[t][12:]
+        return remote(buf1.at[k, me], late_ref.at[span_of(k, t, slot)], ss.at[k * n1 + p],
+                      rs.at[k * n1 + slot], dev(p))
+
+    def keep(k, t):
+        me, buf1 = kinds[t][1], kinds[t][6]
+        return pltpu.make_async_copy(buf1.at[k, me], late_ref.at[span_of(k, t, me)],
+                                     put_sem.at[k * 2 + t])
+
+    def share(k, which):
+        rows = pl.ds(pl.multiple_of(k * chunk + which * half, half), half)
+        return remote(late_ref.at[rows], late_ref.at[rows], p5s.at[k], p5r.at[k], sibling)
+
+    def peers_of(n, me):
+        return [lax.rem(me + d, n) for d in range(1, n)]
+
+    def product(k):
+        def run(which, dst, add):
+            start = pl.multiple_of(k * chunk + which * half, half)
+            lhs = act_ref[:, pl.ds(start, half)].T
+
+            @pl.loop(0, wide // step)
+            def _(i):
+                cols = pl.ds(pl.multiple_of(i * step, step), step)
+                block = jnp.dot(lhs, gh_ref[:, cols], preferred_element_type=f32)
+                if add:
+                    block = block + dst[k, :, cols].astype(f32)
+                dst[k, :, cols] = block.astype(bf16)
+
+        run(1 - core, give, False)
+        to_pair(k).start()
+        to_own = k - 1
+        return run, to_own
+
+    def own_product(k, run):
+        to_pair(k).wait_recv()
+        run(core, held, True)
+        for t in range(2):
+            n1, me = kinds[t][:2]
+            for p in peers_of(n1, me):
+                first(k, t, p, me).start()
+
+    waiting = None
+    for k in range(CHUNKS):
+        run, _ = product(k)
+        if waiting is not None:
+            own_product(k - 1, waiting)
+        waiting = run
+    own_product(CHUNKS - 1, waiting)
+
+    def scatter_done(k):
+        for t in range(2):
+            n1, me, _, n2, me2, _, buf1, buf2 = kinds[t][:8]
+            sub = tall // n1
+            total = held[k, pl.ds(pl.multiple_of(t * tall + me * sub, sub), sub)].astype(f32)
+            for p in peers_of(n1, me):
+                first(k, t, p, p).wait_recv()
+                total = total + buf1[k, p].astype(f32)
+            buf2[k, me2] = total.astype(bf16)
+            for q in peers_of(n2, me2):
+                second(k, t, q, me2).start()
+
+    def sum_done(k):
+        for t in range(2):
+            n1, me, _, n2, me2, _, buf1, buf2 = kinds[t][:8]
+            for q in peers_of(n2, me2):
+                second(k, t, q, q).wait_recv()
+            total = buf2[k, 0].astype(f32)
+            for j in range(1, n2):
+                total = total + buf2[k, j].astype(f32)
+            buf1[k, me] = total.astype(bf16)
+            for p in peers_of(n1, me):
+                third(k, t, p, me).start()
+            keep(k, t).start()
+
+    def gather_done(k):
+        for t in range(2):
+            n1, me = kinds[t][:2]
+            for p in peers_of(n1, me):
+                third(k, t, p, p).wait_recv()
+            keep(k, t).wait()
+        share(k, core).start()
+
+    for load in loads:
+        load.wait()
+    buf[b] = jnp.zeros(buf.shape[1:], f32)
+    lane = 256
+    tile = 512
+
+    def sig(v):
+        return 1.0 / (1.0 + jnp.exp(-v))
+
+    def chain(i):
+        cols = pl.ds(pl.multiple_of(i * lane, lane), lane)
+        mean, rstd = vec_ref[0:1, cols], vec_ref[1:2, cols]
+        gain, bias = vec_ref[2:3, cols], vec_ref[3:4, cols]
+
+        @pl.loop(0, images // tile)
+        def _(j):
+            rows = pl.ds(pl.multiple_of(j * tile, tile), tile)
+            grad = lax.dot_general(
+                gh_ref[rows, :], w_ref[cols, :], (((1,), (1,)), ((), ())),
+                preferred_element_type=f32,
+            )
+            normed = (raw_ref[rows, cols].astype(f32) - mean) * rstd
+            pre = normed * gain + bias
+            gate = sig(pre)
+            grad = grad * (gate * (1.0 + pre * (1.0 - gate)))
+            buf[b, 0:1, cols] += jnp.sum(grad, 0, keepdims=True)
+            buf[b, 1:2, cols] += jnp.sum(grad * normed, 0, keepdims=True)
+            gact[rows, cols] = grad.astype(bf16)
+
+    tiles = mid // lane
+    for k in range(CHUNKS):
+        @pl.loop(k * tiles // CHUNKS, (k + 1) * tiles // CHUNKS)
+        def _(i):
+            chain(i)
+
+        scatter_done(k)
+
+    sums = exchange(n_batch, buf, sum_send, sum_recv)
+    count = images * n_batch
+    buf[b] = sums / count
+
+    @pl.loop(0, mid // lane)
+    def _(i):
+        cols = pl.ds(pl.multiple_of(i * lane, lane), lane)
+        mean, rstd, gain = vec_ref[0:1, cols], vec_ref[1:2, cols], vec_ref[2:3, cols]
+        one, two = buf[b, 0:1, cols], buf[b, 1:2, cols]
+
+        @pl.loop(0, images // lane)
+        def _(j):
+            rows = pl.ds(pl.multiple_of(j * lane, lane), lane)
+            normed = (raw_ref[rows, cols].astype(f32) - mean) * rstd
+            grad = gact[rows, cols].astype(f32)
+            gact[rows, cols] = (gain * rstd * (grad - one - normed * two)).astype(bf16)
+
+    rows, width = early_ref.shape
     span = rows * n_batch
-    step = min(width, 512)
-
+    step_e = min(width, 512)
     order = []
     for i in range(n_chan // 2):
         order += [i, n_chan - 1 - i]
-    for d in order:
+
+    def early_part(d):
         lhs = jnp.concatenate(
             [x_ref[:, (k * n_chan + d) * span:(k * n_chan + d + 1) * span] for k in range(n_sec)], 1
         ).T
 
-        @pl.loop(0, width // step)
+        @pl.loop(0, width // step_e)
         def _(i):
-            cols = pl.ds(pl.multiple_of(i * step, step), step)
-            block = jnp.dot(lhs, g_ref[:, cols], preferred_element_type=jnp.float32)
-            part[d, :, :, :, :, cols] = block.reshape(n_sec, n_y, 2, rows, step).astype(jnp.bfloat16)
-
-        remote(part.at[d, :, :, 1 - core], pair.at[d], pair_send.at[d], pair_recv.at[d],
-               sibling).start()
+            cols = pl.ds(pl.multiple_of(i * step_e, step_e), step_e)
+            block = jnp.dot(lhs, gact[:, cols], preferred_element_type=f32)
+            part[d, :, :, :, :, cols] = block.reshape(n_sec, n_y, 2, rows, step_e).astype(bf16)
+
+        pair_copy(d).start()
+
+    def pair_copy(d):
+        return remote(part.at[d, :, :, 1 - core], pair.at[d], pair_send.at[d], pair_recv.at[d], sibling)
 
     def from_pair(d):
-        remote(part.at[d, :, :, 1 - core], pair.at[d], pair_send.at[d], pair_recv.at[d],
-               sibling).wait_recv()
-        mine[d] = (
-            part[d, :, :, core].astype(jnp.float32) + pair[d].astype(jnp.float32)
-        ).astype(jnp.bfloat16)
+        pair_copy(d).wait_recv()
+        mine[d] = (part[d, :, :, core].astype(f32) + pair[d].astype(f32)).astype(bf16)
 
     def lower(d):
         return remote(mine.at[d], low.at[d], low_send.at[d], low_recv.at[d],
@@ -273,9 +467,9 @@
                       {"chan": lax.rem(z + 1, n_chan)})
 
     def add(d, arrived):
-        mine[d] = (mine[d].astype(jnp.float32) + arrived[d].astype(jnp.float32)).astype(jnp.bfloat16)
-
-    for d in order:
+        mine[d] = (mine[d].astype(f32) + arrived[d].astype(f32)).astype(bf16)
+
+    def ready(d):
         from_pair(d)
 
         @pl.when(jnp.logical_and(z == n_chan - 1, d < z))
@@ -286,6 +480,16 @@
         def _():
             upper(d).start()
 
+    for n, d in enumerate(order):
+        early_part(d)
+        if n > 0:
+            ready(order[n - 1])
+    ready(order[-1])
+    sum_done(0)
+    sum_done(1)
+
+    later = [lambda k=k: sum_done(k) for k in range(2, CHUNKS)]
+    later += [lambda k=k: gather_done(k) for k in range(CHUNKS)]
     for i in range(n_chan):
         d, e = i, n_chan - 1 - i
 
@@ -306,21 +510,27 @@
             @pl.when(e > z)
             def _():
                 upper(e).start()
+
+        if i < 2:
+            for act_now in later[:2]:
+                act_now()
+            later = later[2:]
 
     slot = s * n_y + y
     for p, q in plane:
         remote(mine.at[z, p, q], last.at[slot], last_send.at[p * n_y + q], last_recv.at[slot],
                {"section": p, "batch": q * 2 + core}).start()
-    total = mine[z, s, y].astype(jnp.float32)
+    for act_now in later:
+        act_now()
+    total = mine[z, s, y].astype(f32)
     for p, q in plane:
         there = p * n_y + q
         remote(mine.at[z, p, q], last.at[there], last_send.at[there], last_recv.at[there],
                {"section": p, "batch": q * 2 + core}).wait()
-        total = total + last[there].astype(jnp.float32)
-    o_ref[...] = total
+        total = total + last[there].astype(f32)
+    early_ref[...] = total
     for d in range(n_chan):
-        remote(part.at[d, :, :, 1 - core], pair.at[d], pair_send.at[d], pair_recv.at[d],
-               sibling).wait_send()
+        pair_copy(d).wait_send()
 
         @pl.when(d < z)
         def _():
@@ -330,28 +540,61 @@
         def _():
             upper(d).wait_send()
 
-
-def early_gradient(x, g, collective_id):
+    for k in range(CHUNKS):
+        share(k, 1 - core).wait_recv()
+        share(k, core).wait_send()
+        to_pair(k).wait_send()
+        for t in range(2):
+            n1, me, _, n2, me2 = kinds[t][:5]
+            for p in peers_of(n1, me):
+                first(k, t, p, me).wait_send()
+                third(k, t, p, me).wait_send()
+            for q in peers_of(n2, me2):
+                second(k, t, q, me2).wait_send()
+
+
+def backward(act, grad_h, vectors, w_late, raw, x, collective_id):
     n_sec, n_chan, n_batch = (lax.axis_size(a) for a in ("section", "chan", "batch"))
     n_y = n_batch // 2
-    width = g.shape[1]
+    mid, wide = w_late.shape
     rows = x.shape[1] // (n_sec * n_chan * n_batch)
-    quarter = (n_chan, n_sec, n_y, rows, width)
+    quarter = (n_chan, n_sec, n_y, rows, mid)
+    half, tall = mid // CHUNKS // 2, mid // CHUNKS // 4
+    bf16 = jnp.bfloat16
+    vmem, anywhere = pl.BlockSpec(memory_space=pltpu.VMEM), pl.BlockSpec(memory_space=pl.ANY)
+    sems = [3, 2 * CHUNKS, CHUNKS, CHUNKS]
+    sems += [CHUNKS * n for n in (n_sec, n_sec, n_y, n_y, n_y, n_y, n_sec, n_sec, n_sec, n_sec, n_y, n_y)]
+    sems += [CHUNKS, CHUNKS, n_batch, n_batch] + [n_chan] * 6 + [n_sec * n_y] * 2
     return pl.pallas_call(
-        functools.partial(early_grad_kernel, n_sec, n_chan, n_batch),
-        out_shape=jax.ShapeDtypeStruct((rows, width), jnp.float32),
-        in_specs=[pl.BlockSpec(memory_space=pltpu.VMEM)] * 2,
-        out_specs=pl.BlockSpec(memory_space=pltpu.VMEM),
-        scratch_shapes=[pltpu.VMEM((n_chan, n_sec, n_y, 2, rows, width), jnp.bfloat16)]
-        + [pltpu.VMEM(quarter, jnp.bfloat16)] * 4
-        + [pltpu.VMEM((n_sec * n_y, rows, width), jnp.bfloat16)]
-        + [pltpu.SemaphoreType.DMA((n_chan,))] * 6
-        + [pltpu.SemaphoreType.DMA((n_sec * n_y,))] * 2,
+        functools.partial(backward_kernel, n_sec, n_chan, n_batch),
+        out_shape=(
+            jax.ShapeDtypeStruct((mid, wide), bf16),
+            jax.ShapeDtypeStruct((rows, mid), jnp.float32),
+        ),
+        in_specs=[vmem, vmem, vmem, anywhere, anywhere, anywhere],
+        out_specs=[anywhere, vmem],
+        scratch_shapes=[
+            pltpu.VMEM(w_late.shape, bf16),
+            pltpu.VMEM(raw.shape, bf16),
+            pltpu.VMEM(x.shape, bf16),
+            pltpu.VMEM((CHUNKS, half, wide), bf16),
+            pltpu.VMEM((CHUNKS, half, wide), bf16),
+            pltpu.VMEM(raw.shape, bf16),
+            pltpu.VMEM((n_batch, 8, mid), jnp.float32),
+            pltpu.VMEM((CHUNKS, n_sec, tall // n_sec, wide), bf16),
+            pltpu.VMEM((CHUNKS, n_y, tall // n_y, wide), bf16),
+            pltpu.VMEM((CHUNKS, n_y, tall // n_sec, wide), bf16),
+            pltpu.VMEM((CHUNKS, n_sec, tall // n_y, wide), bf16),
+            pltpu.VMEM((n_chan, n_sec, n_y, 2, rows, mid), bf16),
+        ]
+        + [pltpu.VMEM(quarter, bf16)] * 4
+        + [pltpu.VMEM((n_sec * n_y, rows, mid), bf16)]
+        + [pltpu.SemaphoreType.DMA((n,)) for n in sems],
         compiler_params=pltpu.CompilerParams(
-            collective_id=collective_id, has_side_effects=True, vmem_limit_bytes=56 * 2**20
+            collective_id=collective_id, has_side_effects=True, vmem_limit_bytes=63 * 2**20
         ),
-        name="early_gradient",
-    )(x, g)
+        name="backward",
+    )(act, grad_h, vectors, w_late, raw, x)
 
 
 def body(images, w_early, gain_early, bias_early, w_late, gain_late, bias_late, cotangent):
@@ -384,23 +627,9 @@
         gain_late * rstd_l * (grad_y - back_one / total_rows - normed_l * (back_two / total_rows))
     ).astype(jnp.bfloat16)
 
-    part_late = lax.dot_general(
-        act, grad_h, (((0,), (0,)), ((), ())), preferred_element_type=jnp.float32
-    ).astype(jnp.bfloat16)
-    part_late, grad_h = lax.optimization_barrier((part_late, grad_h))
-    grad_late = lax.psum(part_late, ("section", "batch")).astype(jnp.float32)
-
-    grad_act = lax.dot_general(
-        grad_h, w_late, (((1,), (1,)), ((), ())), preferred_element_type=jnp.float32
-    )
-    grad_pre = grad_act * smooth_slope(pre_e)
-    early_one, early_two = batch_sums(jnp.sum(grad_pre, 0), jnp.sum(grad_pre * normed_e, 0), 3)
-    grad_raw = (
-        gain_early
-        * rstd_e
-        * (grad_pre - early_one / total_rows - normed_e * (early_two / total_rows))
-    ).astype(jnp.bfloat16)
-    grad_early = early_gradient(flat_in, grad_raw, 4)
+    vectors = jnp.pad(jnp.stack([mean_e, rstd_e, gain_early, bias_early]), ((0, 4), (0, 0)))
+    grad_late, grad_early = backward(act, grad_h, vectors, w_late, raw, flat_in, 4)
+    grad_late = grad_late.astype(jnp.float32)
     return (late_out, grad_late, grad_early)
 
 

time: 274 us -> 256 us (0.934)
  Pallas kernels: 153 us -> 203 us
  matrix products: 47.8 us -> 11.1 us
  between operations: 14.1 us -> 0.75 us
  waiting for transfers between devices: 12.4 us -> 0 us
    pallas_call x1, Pallas kernels: 93.9 us -> 150 us  [backward(): pl.pallas_call(functools.partial(backward_kernel, n_sec, n_chan, n_batch)...]
    dot_general x2 -> x0, matrix products: 31.2 us -> none  [the longest x1 18.3 us: body(): lax.dot_general(grad_h, w_late, (((1,), (1,)), ((), ())), preferred_eleme...]
    psum x1 -> x0, waiting for transfers between devices: 12.3 us -> none  [body(): grad_late = lax.psum(part_late, ('section', 'batch')).astype(jnp.float32)]
    pallas_call x3 -> x2, Pallas kernels: 19.1 us -> 12.7 us  [batch_sums(): pl.pallas_call(functools.partial(sums_kernel, n), out_shape=jax.ShapeDtyp...]
    dot_general x1, matrix products: 16.5 us -> 11.1 us  [body(): late = jnp.dot(act, w_late, preferred_element_type=jnp.float32)]
    convert_element_type x2, other arithmetic: 19.2 us -> 16.2 us  [the longest x1 11.7 us: body(): grad_late = grad_late.astype(jnp.float32)]
  transfers between devices with their start and end apart: 1 -> 0, of which waited for: 1 -> 0; matrix products, arithmetic and copies ran while one was open for 10% -> 0% of each run, Pallas kernels for 37% -> 0%
where the time goes in v3:
time: 256 us; the launch traced here: 255 us
  Pallas kernels  203 us (79%)
  other arithmetic  40.2 us (16%)
  matrix products  11.1 us (4%)
    pallas_call x1, Pallas kernels, backward(): pl.pallas_call(functools.partial(backward_kernel, n_sec, n_chan, n_batch)...  150 us
    pallas_call x1, Pallas kernels, early_forward(): pl.pallas_call(functools.partial(early_kernel, n_chan, n_batch), out_shap...  40.3 us
    pallas_call x2, Pallas kernels, batch_sums(): pl.pallas_call(functools.partial(sums_kernel, n), out_shape=jax.ShapeDtyp...  12.7 us
    convert_element_type x1, other arithmetic, body(): grad_late = grad_late.astype(jnp.float32)  11.7 us
    dot_general x1, matrix products, body(): late = jnp.dot(act, w_late, preferred_element_type=jnp.float32)  11.1 us
    convert_element_type x1, other arithmetic, body(): grad_h = (gain_late * rstd_l * (grad_y - back_one / total_rows - normed_l...  10.4 us
    reduce_sum x1, other arithmetic, body(): jnp.sum(grad_y, 0)  7.55 us

profile of v3, /device:TPU:19, one launch (start us, length us, event | category | flops | bytes accessed | tf_op | source)
XLA Modules:
  0.0 255.4 jit_solution(8343707667471032843)
XLA Ops:
  0.6 40.3 %early_forward.1 = (bf16[1024,1024]{1,0:T(8,128)(2,1)}, bf16[1024,2048]{1,0:T(8,128)(2,1)}, f32[8,2048]{1,0:T(8,128)}) custom-call(bf16[256,1024]{1,0:T(8,128)(2,1)} %bitcast.40, bf16[1024,2048]{1,0:T(8,128)(2,1)} %w_ref.1), custom_call_target="tpu_custom_call" | custom-call | tf_op jit(solution)/shard_map/early_forward/pallas_call | solution.py:204
  41.0 0.0 copy-start.1
  41.0 1.0 slice_multiply_fusion.1
  42.0 1.6 select_maximum_fusion.vec_ref
  43.6 4.5 %multiply_convert_fusion.2.act_ref = bf16[1024,2048]{1,0:T(8,128)(2,1)S(1)} fusion(bf16[1024,2048]{1,0:T(8,128)(2,1)} %get-tuple-element.8.raw_hbm, f32[2048]{0:T(1024)} %param.11, f32[2048]{0:T(1024)} %param.10, f32[2048]{0:T(1024)S(1)} %bitcast.42, f32[2048]{0:T(1024)S(1)} %bitcast.41), kind=kLoop, calls=%fused_computation.8 | loop fusion | flops 20971520 | bytes 8421376 | tf_op jit(solution)/shard_map/convert_element_type | solution.py:615
  48.1 0.0 copy-done.1
  48.2 0.0 copy-start
  48.2 0.0 copy-start.3
  48.2 0.0 copy-start.4
  48.2 11.1 %fusion.4 = (f32[2048]{0:T(1024)S(1)}, f32[2048]{0:T(1024)S(1)}, f32[1024,2048]{1,0:T(8,128)}) fusion(bf16[1024,2048]{1,0:T(8,128)(2,1)S(1)} %multiply_convert_fusion.2.act_ref, bf16[2048,2048]{1,0:T(8,128)(2,1)S(1)} %copy-done.1), kind=kOutput, calls=%fused_computation.26 | convolution fusion | flops 8596221952 | bytes 20987904 | tf_op jit(solution)/shard_map/dot_general | solution.py:617
  59.3 0.0 copy-done
  59.3 0.6 pad_maximum_fusion.x_ref
  59.9 7.6 %batch_sums_1.1 = f32[32,128]{1,0:T(8,128)} custom-call(f32[32,128]{1,0:T(8,128)} %pad_maximum_fusion.x_ref), custom_call_target="tpu_custom_call" | custom-call | tf_op jit(solution)/shard_map/batch_sums_1/pallas_call | solution.py:63
  67.5 0.7 multiply_bitcast_fusion.2
  68.2 0.0 copy-done.3
  68.2 0.7 fusion.2
  68.9 0.0 copy-done.4
  68.9 7.5 %fusion.3 = (f32[2048]{0:T(1024)S(1)}, f32[2048]{0:T(1024)S(1)}) fusion(f32[2048]{0:T(1024)S(1)} %copy-done.4, f32[2048]{0:T(1024)S(1)} %copy-done.3, f32[2048]{0:T(1024)S(1)} %get-tuple-element.22, f32[1024,2048]{1,0:T(8,128)} %get-tuple-element.25, f32[2048]{0:T(1024)S(1)} %multiply_bitcast_fusion.2, bf16[1,4,256,2048]{3,2,1,0:T(8,128)(2,1)} %param.15), kind=kLoop, calls=%fused_computation.25 | loop fusion | flops 33550336 | bytes 12632064 | tf_op jit(solution)/shard_map/reduce_sum | solution.py:625
  76.5 0.6 pad_maximum_fusion.1.x_ref
  77.1 5.1 %batch_sums_2.1 = f32[32,128]{1,0:T(8,128)} custom-call(f32[32,128]{1,0:T(8,128)} %pad_maximum_fusion.1.x_ref), custom_call_target="tpu_custom_call" | custom-call | tf_op jit(solution)/shard_map/batch_sums_2/pallas_call | solution.py:63
  82.2 0.7 multiply_bitcast_fusion.1
  82.9 10.4 %multiply_convert_fusion = (bf16[1024,2048]{1,0:T(8,128)(2,1)}, bf16[1024,2048]{1,0:T(8,128)(2,1)}) fusion(f32[1024,2048]{1,0:T(8,128)} %get-tuple-element.25, f32[2048]{0:T(1024)S(1)} %get-tuple-element.24, f32[2048]{0:T(1024)S(1)} %get-tuple-element.23, f32[2048]{0:T(1024)S(1)} %get-tuple-element.21, f32[2048]{0:T(1024)S(1)} %get-tuple-element.22, ...), kind=kLoop, calls=%fused_computation.1 | loop fusion | flops 41943040 | bytes 21028864 | tf_op jit(solution)/shard_map/convert_element_type | solution.py:628
  93.3 149.7 %backward.1 = (bf16[2048,2048]{1,0:T(8,128)(2,1)}, f32[32,2048]{1,0:T(8,128)}) custom-call(bf16[1024,2048]{1,0:T(8,128)(2,1)} %copy-done, bf16[1024,2048]{1,0:T(8,128)(2,1)} %get-tuple-element.17.gh_ref, f32[8,2048]{1,0:T(8,128)} %select_maximum_fusion.vec_ref, bf16[2048,2048]{1,0:T(8,128)(2,1)} %w_hbm.1, bf16[1024,2048]{1,0:T(8,128)(2,1)} %get-tuple-element.8.raw_hbm, ...), custom_call_target="tpu_custom_call" | custom-call | tf_op jit(solution)/shard_map/backward/pallas_call | solution.py:568
  243.0 0.0 copy-start.2
  243.0 11.7 %convert_element_type.29 = f32[2048,2048]{1,0:T(8,128)} convert(bf16[2048,2048]{1,0:T(8,128)(2,1)} %get-tuple-element.11) | non-fusion elementwise | flops 4194304 | bytes 25165824 | tf_op jit(solution)/shard_map/convert_element_type | solution.py:632
  254.7 0.0 copy-done.2
  254.7 0.7 copy.12
Async XLA Ops:
  41.0 7.2 %copy-start.1 = (bf16[2048,2048]{1,0:T(8,128)(2,1)S(1)}, bf16[2048,2048]{1,0:T(8,128)(2,1)}, u32[]{:S(2)}) copy-start(bf16[2048,2048]{1,0:T(8,128)(2,1)} %w_hbm.1) | copy-start | bytes 25165828
  48.2 11.1 %copy-start = (bf16[1024,2048]{1,0:T(8,128)(2,1)}, bf16[1024,2048]{1,0:T(8,128)(2,1)S(1)}, u32[]{:S(2)}) copy-start(bf16[1024,2048]{1,0:T(8,128)(2,1)S(1)} %multiply_convert_fusion.2.act_ref) | copy-start | bytes 12582916
  48.2 20.0 %copy-start.3 = (f32[2048]{0:T(1024)S(1)}, f32[2048]{0:T(1024)}, u32[]{:S(2)}) copy-start(f32[2048]{0:T(1024)} %param.13) | copy-start | bytes 24580
  48.2 20.7 %copy-start.4 = (f32[2048]{0:T(1024)S(1)}, f32[2048]{0:T(1024)}, u32[]{:S(2)}) copy-start(f32[2048]{0:T(1024)} %param.14) | copy-start | bytes 24580
  243.0 11.7 %copy-start.2 = (f32[32,2048]{1,0:T(8,128)S(1)}, f32[32,2048]{1,0:T(8,128)}, u32[]{:S(2)}) copy-start(f32[32,2048]{1,0:T(8,128)} %get-tuple-element.31) | copy-start | bytes 786436

commit v4 on v3

--- a/solution.py
+++ b/solution.py
@@ -8,73 +8,6 @@
 from jax.sharding import PartitionSpec as P
 
 MESH = pl.DeviceIdType.MESH
-
-
-def smooth_gate(values):
-    return values * jax.nn.sigmoid(values)
-
-
-def smooth_slope(values):
-    sig = jax.nn.sigmoid(values)
-    return sig * (1.0 + values * (1.0 - sig))
-
-
-def sums_kernel(n, x_ref, o_ref, buf, send_sem, recv_sem):
-    me = lax.axis_index("batch")
-    peers = [lax.rem(me + d, n) for d in range(1, n)]
-    barrier = pltpu.get_barrier_semaphore()
-    for peer in peers:
-        pl.semaphore_signal(barrier, inc=1, device_id={"batch": peer}, device_id_type=MESH)
-    buf[me] = x_ref[...]
-    pl.semaphore_wait(barrier, n - 1)
-    copies = []
-    for peer in peers:
-        copy = pltpu.make_async_remote_copy(
-            src_ref=x_ref,
-            dst_ref=buf.at[me],
-            send_sem=send_sem.at[peer],
-            recv_sem=recv_sem.at[me],
-            device_id={"batch": peer},
-            device_id_type=MESH,
-        )
-        copy.start()
-        copies.append(copy)
-    for peer in peers:
-        pltpu.make_async_remote_copy(
-            src_ref=x_ref,
-            dst_ref=buf.at[peer],
-            send_sem=send_sem.at[peer],
-            recv_sem=recv_sem.at[peer],
-            device_id={"batch": peer},
-            device_id_type=MESH,
-        ).wait_recv()
-    total = buf[0]
-    for k in range(1, n):
-        total = total + buf[k]
-    o_ref[...] = total
-    for copy in copies:
-        copy.wait_send()
-
-
-def batch_sums(one, two, collective_id):
-    n = lax.axis_size("batch")
-    width = one.shape[0]
-    x = jnp.concatenate([one, two]).reshape(-1, 128)
-    out = pl.pallas_call(
-        functools.partial(sums_kernel, n),
-        out_shape=jax.ShapeDtypeStruct(x.shape, x.dtype),
-        in_specs=[pl.BlockSpec(memory_space=pltpu.VMEM)],
-        out_specs=pl.BlockSpec(memory_space=pltpu.VMEM),
-        scratch_shapes=[
-            pltpu.VMEM((n,) + x.shape, x.dtype),
-            pltpu.SemaphoreType.DMA((n,)),
-            pltpu.SemaphoreType.DMA((n,)),
-        ],
-        compiler_params=pltpu.CompilerParams(collective_id=collective_id, has_side_effects=True),
-        name=f"batch_sums_{collective_id}",
-    )(x)
-    out = out.reshape(2, width)
-    return out[0], out[1]
 
 
 def meet(groups):
@@ -224,11 +157,139 @@
 
 
 CHUNKS = 4
+STRIP = 64
+
+
+def half_gate(v):
+    return 0.5 * jnp.tanh(0.5 * v) + 0.5
+
+
+def fold(v):
+    return jnp.sum(v.reshape(-1, 8, v.shape[1]), 0)
+
+
+def late_kernel(n_batch, raw_ref, vec_ref, lvec_ref, w_ref, cot_hbm, act_ref, out_ref, gh_ref,
+                cot_ref, hidden, grad_y, buf, back, cot_sem, sum_send, sum_recv, back_send, back_recv):
+    b = lax.axis_index("batch")
+    load = pltpu.make_async_copy(cot_hbm, cot_ref, cot_sem)
+    load.start()
+    meet([{"batch": p} for p in others("batch", n_batch)])
+    f32, bf16 = jnp.float32, jnp.bfloat16
+    rows, mid = raw_ref.shape
+    wide = w_ref.shape[1]
+    lane = 256
+    buf[b] = jnp.zeros(buf.shape[1:], f32)
+
+    @pl.loop(0, mid // lane)
+    def _(i):
+        cols = pl.ds(pl.multiple_of(i * lane, lane), lane)
+        scale = vec_ref[1:2, cols] * vec_ref[2:3, cols]
+        shift = vec_ref[3:4, cols] - vec_ref[0:1, cols] * scale
+
+        def strip(r, carry):
+            here = pl.ds(pl.multiple_of(r * STRIP, STRIP), STRIP)
+            pre = raw_ref[here, cols].astype(f32) * scale + shift
+            act_ref[here, cols] = (pre * half_gate(pre)).astype(bf16)
+            return carry
+
+        lax.fori_loop(0, rows // STRIP, strip, 0, unroll=2)
+
+    tile = 512
+
+    @pl.loop(0, wide // lane)
+    def _(i):
+        cols = pl.ds(pl.multiple_of(i * lane, lane), lane)
+
+        @pl.loop(0, rows // tile)
+        def _(j):
+            here = pl.ds(pl.multiple_of(j * tile, tile), tile)
+            block = jnp.dot(act_ref[here, :], w_ref[:, cols], preferred_element_type=f32)
+            hidden[here, cols] = block
+            buf[b, 0:1, cols] += jnp.sum(block, 0, keepdims=True)
+            buf[b, 1:2, cols] += jnp.sum(block * block, 0, keepdims=True)
+
+    sums = exchange(n_batch, buf, sum_send, sum_recv)
+    count = rows * n_batch
+    mean = sums[0:1] / count
+    buf[b, 0:1] = mean
+    buf[b, 1:2] = lax.rsqrt(sums[1:2] / count - mean * mean + 1e-05)
+    load.wait()
+
+    @pl.loop(0, wide // lane)
+    def _(i):
+        cols = pl.ds(pl.multiple_of(i * lane, lane), lane)
+        mean, rstd = buf[b, 0:1, cols], buf[b, 1:2, cols]
+        gain, bias = lvec_ref[0:1, cols], lvec_ref[1:2, cols]
+
+        def strip(r, sums):
+            here = pl.ds(pl.multiple_of(r * STRIP, STRIP), STRIP)
+            normed = (hidden[here, cols] - mean) * rstd
+            pre = normed * gain + bias
+            gate = half_gate(pre)
+            out_ref[here, cols] = (pre * gate).astype(bf16)
+            grad = cot_ref[here, cols].astype(f32) * (gate * (1.0 + pre * (1.0 - gate)))
+            hidden[here, cols] = normed
+            grad_y[here, cols] = grad
+            return sums[0] + fold(grad), sums[1] + fold(grad * normed)
+
+        zero = jnp.zeros((8, lane), f32)
+        one, two = lax.fori_loop(0, rows // STRIP, strip, (zero, zero), unroll=2)
+        back[b, :, cols] = jnp.concatenate(
+            [jnp.sum(one, 0, keepdims=True), jnp.sum(two, 0, keepdims=True), zero[:6]], 0
+        )
+
+    back[b] = exchange(n_batch, back, back_send, back_recv) / count
+
+    @pl.loop(0, wide // lane)
+    def _(i):
+        cols = pl.ds(pl.multiple_of(i * lane, lane), lane)
+        scale = buf[b, 1:2, cols] * lvec_ref[0:1, cols]
+        one, two = back[b, 0:1, cols], back[b, 1:2, cols]
+
+        def strip(r, carry):
+            here = pl.ds(pl.multiple_of(r * STRIP, STRIP), STRIP)
+            gh_ref[here, cols] = (
+                scale * (grad_y[here, cols] - one - hidden[here, cols] * two)
+            ).astype(bf16)
+            return carry
+
+        lax.fori_loop(0, rows // STRIP, strip, 0, unroll=2)
+
+
+def late_layer(raw, vectors, late_vectors, w_late, cotangent, collective_id):
+    n_batch = lax.axis_size("batch")
+    rows = raw.shape[0]
+    mid, wide = w_late.shape
+    vmem, anywhere = pl.BlockSpec(memory_space=pltpu.VMEM), pl.BlockSpec(memory_space=pl.ANY)
+    f32, bf16 = jnp.float32, jnp.bfloat16
+    return pl.pallas_call(
+        functools.partial(late_kernel, n_batch),
+        out_shape=(
+            jax.ShapeDtypeStruct((rows, mid), bf16),
+            jax.ShapeDtypeStruct((rows, wide), bf16),
+            jax.ShapeDtypeStruct((rows, wide), bf16),
+        ),
+        in_specs=[vmem] * 4 + [anywhere],
+        out_specs=[vmem] * 3,
+        scratch_shapes=[
+            pltpu.VMEM((rows, wide), bf16),
+            pltpu.VMEM((rows, wide), f32),
+            pltpu.VMEM((rows, wide), f32),
+            pltpu.VMEM((n_batch, 8, wide), f32),
+            pltpu.VMEM((n_batch, 8, wide), f32),
+            pltpu.SemaphoreType.DMA,
+        ]
+        + [pltpu.SemaphoreType.DMA((n_batch,))] * 4,
+        compiler_params=pltpu.CompilerParams(
+            collective_id=collective_id, has_side_effects=True, vmem_limit_bytes=62 * 2**20
+        ),
+        name="late_layer",
+    )(raw, vectors, late_vectors, w_late, cotangent)
 
 
 def backward_kernel(n_sec, n_chan, n_batch, act_ref, gh_ref, vec_ref, w_hbm, raw_hbm, x_hbm,
                     late_ref, early_ref, w_ref, raw_ref, x_ref, give, held, gact, buf,
-                    fa, fb, sa, sb, part, pair, mine, low, high, last,
+                    fa, fb, sa, sb, part, pair, mine, low, high, last, square,
                     load_sem, put_sem, p1s, p1r, fas, far, fbs, fbr, sas, sar, sbs, sbr,
                     cas, car, cbs, cbr, p5s, p5r, sum_send, sum_recv,
                     pair_send, pair_recv, low_send, low_recv, high_send, high_recv,
@@ -325,8 +386,7 @@
 
         run(1 - core, give, False)
         to_pair(k).start()
-        to_own = k - 1
-        return run, to_own
+        return run
 
     def own_product(k, run):
         to_pair(k).wait_recv()
@@ -338,7 +398,7 @@
 
     waiting = None
     for k in range(CHUNKS):
-        run, _ = product(k)
+        run = product(k)
         if waiting is not None:
             own_product(k - 1, waiting)
         waiting = run
@@ -383,9 +443,6 @@
     lane = 256
     tile = 512
 
-    def sig(v):
-        return 1.0 / (1.0 + jnp.exp(-v))
-
     def chain(i):
         cols = pl.ds(pl.multiple_of(i * lane, lane), lane)
         mean, rstd = vec_ref[0:1, cols], vec_ref[1:2, cols]
@@ -394,17 +451,25 @@
         @pl.loop(0, images // tile)
         def _(j):
             rows = pl.ds(pl.multiple_of(j * tile, tile), tile)
-            grad = lax.dot_general(
+            square[...] = lax.dot_general(
                 gh_ref[rows, :], w_ref[cols, :], (((1,), (1,)), ((), ())),
                 preferred_element_type=f32,
             )
-            normed = (raw_ref[rows, cols].astype(f32) - mean) * rstd
-            pre = normed * gain + bias
-            gate = sig(pre)
-            grad = grad * (gate * (1.0 + pre * (1.0 - gate)))
-            buf[b, 0:1, cols] += jnp.sum(grad, 0, keepdims=True)
-            buf[b, 1:2, cols] += jnp.sum(grad * normed, 0, keepdims=True)
-            gact[rows, cols] = grad.astype(bf16)
+
+            def strip(r, sums):
+                here = pl.ds(pl.multiple_of(j * tile + r * STRIP, STRIP), STRIP)
+                normed = (raw_ref[here, cols].astype(f32) - mean) * rstd
+                pre = normed * gain + bias
+                gate = half_gate(pre)
+                grad = square[pl.ds(pl.multiple_of(r * STRIP, STRIP), STRIP), :]
+                grad = grad * (gate * (1.0 + pre * (1.0 - gate)))
+                gact[here, cols] = grad.astype(bf16)
+                return sums[0] + fold(grad), sums[1] + fold(grad * normed)
+
+            zero = jnp.zeros((8, lane), f32)
+            one, two = lax.fori_loop(0, tile // STRIP, strip, (zero, zero), unroll=2)
+            buf[b, 0:1, cols] += jnp.sum(one, 0, keepdims=True)
+            buf[b, 1:2, cols] += jnp.sum(two, 0, keepdims=True)
 
     tiles = mid // lane
     for k in range(CHUNKS):
@@ -424,9 +489,9 @@
         mean, rstd, gain = vec_ref[0:1, cols], vec_ref[1:2, cols], vec_ref[2:3, cols]
         one, two = buf[b, 0:1, cols], buf[b, 1:2, cols]
 
-        @pl.loop(0, images // lane)
+        @pl.loop(0, images // STRIP)
         def _(j):
-            rows = pl.ds(pl.multiple_of(j * lane, lane), lane)
+            rows = pl.ds(pl.multiple_of(j * STRIP, STRIP), STRIP)
             normed = (raw_ref[rows, cols].astype(f32) - mean) * rstd
             grad = gact[rows, cols].astype(f32)
             gact[rows, cols] = (gain * rstd * (grad - one - normed * two)).astype(bf16)
@@ -484,9 +549,9 @@
         early_part(d)
         if n > 0:
             ready(order[n - 1])
+        if n == 0 or n == 2:
+            sum_done(n // 2)
     ready(order[-1])
-    sum_done(0)
-    sum_done(1)
 
     later = [lambda k=k: sum_done(k) for k in range(2, CHUNKS)]
     later += [lambda k=k: gather_done(k) for k in range(CHUNKS)]
@@ -588,7 +653,7 @@
             pltpu.VMEM((n_chan, n_sec, n_y, 2, rows, mid), bf16),
         ]
         + [pltpu.VMEM(quarter, bf16)] * 4
-        + [pltpu.VMEM((n_sec * n_y, rows, mid), bf16)]
+        + [pltpu.VMEM((n_sec * n_y, rows, mid), bf16), pltpu.VMEM((512, 256), jnp.float32)]
         + [pltpu.SemaphoreType.DMA((n,)) for n in sems],
         compiler_params=pltpu.CompilerParams(
             collective_id=collective_id, has_side_effects=True, vmem_limit_bytes=63 * 2**20
@@ -599,35 +664,21 @@
 
 def body(images, w_early, gain_early, bias_early, w_late, gain_late, bias_late, cotangent):
     width_in = images.shape[-1]
-    width_mid = w_early.shape[1]
     width_out = w_late.shape[1]
     batch_count = lax.axis_size("batch")
     own = images.reshape(-1, width_in)
     flat_in, raw, sums_e = early_forward(own, w_early, 0)
     total_rows = flat_in.shape[0] * batch_count
 
-    raw_f = raw.astype(jnp.float32)
-    sum_one, sum_two = sums_e[0], sums_e[1]
-    mean_e = sum_one / total_rows
-    rstd_e = lax.rsqrt(sum_two / total_rows - mean_e * mean_e + 1e-05)
-    normed_e = (raw_f - mean_e) * rstd_e
-    pre_e = normed_e * gain_early + bias_early
-    act = smooth_gate(pre_e).astype(jnp.bfloat16)
-
-    late = jnp.dot(act, w_late, preferred_element_type=jnp.float32)
-    late_one, late_two = batch_sums(jnp.sum(late, 0), jnp.sum(late * late, 0), 1)
-    mean_l = late_one / total_rows
-    rstd_l = lax.rsqrt(late_two / total_rows - mean_l * mean_l + 1e-05)
-    normed_l = (late - mean_l) * rstd_l
-    pre_l = normed_l * gain_late + bias_late
-    late_out = smooth_gate(pre_l).astype(jnp.bfloat16).reshape(cotangent.shape)
-    grad_y = cotangent.reshape(-1, width_out).astype(jnp.float32) * smooth_slope(pre_l)
-    back_one, back_two = batch_sums(jnp.sum(grad_y, 0), jnp.sum(grad_y * normed_l, 0), 2)
-    grad_h = (
-        gain_late * rstd_l * (grad_y - back_one / total_rows - normed_l * (back_two / total_rows))
-    ).astype(jnp.bfloat16)
-
+    mean_e = sums_e[0] / total_rows
+    rstd_e = lax.rsqrt(sums_e[1] / total_rows - mean_e * mean_e + 1e-05)
     vectors = jnp.pad(jnp.stack([mean_e, rstd_e, gain_early, bias_early]), ((0, 4), (0, 0)))
+    late_vectors = jnp.pad(jnp.stack([gain_late, bias_late]), ((0, 6), (0, 0)))
+    act, late_out, grad_h = late_layer(
+        raw, vectors, late_vectors, w_late, cotangent.reshape(-1, width_out), 1
+    )
+    late_out = late_out.reshape(cotangent.shape)
+
     grad_late, grad_early = backward(act, grad_h, vectors, w_late, raw, flat_in, 4)
     grad_late = grad_late.astype(jnp.float32)
     return (late_out, grad_late, grad_early)

time: 256 us -> 253 us (0.988)
  Pallas kernels: 203 us -> 236 us
  other arithmetic: 40.2 us -> 13.5 us
  matrix products: 11.1 us -> 0 us
    pallas_call x2 -> x1, Pallas kernels: 12.7 us -> 45.2 us  [late_layer(): pl.pallas_call(functools.partial(late_kernel, n_batch), out_shape=(jax.Sh...]
    convert_element_type x2 -> x0, other arithmetic: 14.9 us -> none  [the longest x1 10.4 us: body(): grad_h = (gain_late * rstd_l * (grad_y - back_one / total_rows - normed_l...]
    dot_general x1 -> x0, matrix products: 11.1 us -> none  [body(): late = jnp.dot(act, w_late, preferred_element_type=jnp.float32)]
    reduce_sum x1 -> x0, other arithmetic: 7.55 us -> none  [body(): jnp.sum(grad_y, 0)]
where the time goes in v4:
time: 253 us
  Pallas kernels  236 us (93%)
  other arithmetic  13.5 us (5%)
  local copies, waits for them, and re-layouts  2.74 us (1%)
    pallas_call x1, Pallas kernels, backward(): pl.pallas_call(functools.partial(backward_kernel, n_sec, n_chan, n_batch)...  150 us
    pallas_call x1, Pallas kernels, late_layer(): pl.pallas_call(functools.partial(late_kernel, n_batch), out_shape=(jax.Sh...  45.2 us
    pallas_call x1, Pallas kernels, early_forward(): pl.pallas_call(functools.partial(early_kernel, n_chan, n_batch), out_shap...  40.3 us
    convert_element_type x1, other arithmetic, body(): grad_late = grad_late.astype(jnp.float32)  11.8 us

profile of v4, /device:TPU:19, one launch (start us, length us, event | category | flops | bytes accessed | tf_op | source)
XLA Modules:
  0.0 252.7 jit_solution(18367407009279252240)
XLA Ops:
  0.6 0.0 copy-start.2
  0.6 0.0 copy-start.3
  0.7 0.0 copy-start.4
  0.7 0.0 copy-start.5
  0.7 40.3 %early_forward.1 = (bf16[1024,1024]{1,0:T(8,128)(2,1)}, bf16[1024,2048]{1,0:T(8,128)(2,1)}, f32[8,2048]{1,0:T(8,128)}) custom-call(bf16[256,1024]{1,0:T(8,128)(2,1)} %bitcast.9, bf16[1024,2048]{1,0:T(8,128)(2,1)} %w_ref.2), custom_call_target="tpu_custom_call" | custom-call | tf_op jit(solution)/shard_map/early_forward/pallas_call | solution.py:137
  41.0 0.9 slice_multiply_fusion
  41.9 0.0 copy-done.2
  41.9 0.0 copy-done.3
  41.9 0.0 copy-done.4
  42.0 0.0 copy-done.5
  42.0 0.7 select_maximum_fusion
  42.7 45.2 %late_layer.1 = (bf16[1024,2048]{1,0:T(8,128)(2,1)}, bf16[1024,2048]{1,0:T(8,128)(2,1)}, bf16[1024,2048]{1,0:T(8,128)(2,1)}) custom-call(bf16[1024,2048]{1,0:T(8,128)(2,1)} %get-tuple-element.11.raw_ref.raw_hbm, f32[8,2048]{1,0:T(8,128)} %get-tuple-element.22.vec_ref, f32[8,2048]{1,0:T(8,128)} %get-tuple-element.21.lvec_ref, bf16[2048,2048]{1,0:T(8,128)(2,1)} %w_hbm.1, ...), custom_call_target="tpu_custom_call" | custom-call | tf_op jit(solution)/shard_map/late_layer/pallas_call | solution.py:265
  87.9 150.3 %backward.1 = (bf16[2048,2048]{1,0:T(8,128)(2,1)}, f32[32,2048]{1,0:T(8,128)}) custom-call(bf16[1024,2048]{1,0:T(8,128)(2,1)} %get-tuple-element.14.act_ref, bf16[1024,2048]{1,0:T(8,128)(2,1)} %get-tuple-element.15.gh_ref, f32[8,2048]{1,0:T(8,128)} %get-tuple-element.22.vec_ref, bf16[2048,2048]{1,0:T(8,128)(2,1)} %w_hbm.1, ...), custom_call_target="tpu_custom_call" | custom-call | tf_op jit(solution)/shard_map/backward/pallas_call | solution.py:633
  238.2 0.0 copy-start
  238.2 11.8 %convert_element_type.7 = f32[2048,2048]{1,0:T(8,128)} convert(bf16[2048,2048]{1,0:T(8,128)(2,1)} %get-tuple-element.17) | non-fusion elementwise | flops 4194304 | bytes 25165824 | tf_op jit(solution)/shard_map/convert_element_type | solution.py:683
  250.0 0.0 copy-done
  250.0 0.0 copy-start.1
  250.0 2.0 copy.13
  252.0 0.0 copy-done.1
  252.0 0.7 copy.14
Async XLA Ops:
  0.6 41.3 %copy-start.2 = (f32[2048]{0:T(1024)S(1)}, f32[2048]{0:T(1024)}, u32[]{:S(2)}) copy-start(f32[2048]{0:T(1024)} %param.14) | copy-start | bytes 24580
  0.6 41.3 %copy-start.3 = (f32[2048]{0:T(1024)S(1)}, f32[2048]{0:T(1024)}, u32[]{:S(2)}) copy-start(f32[2048]{0:T(1024)} %param.13) | copy-start | bytes 24580
  0.7 41.3 %copy-start.4 = (f32[2048]{0:T(1024)S(1)}, f32[2048]{0:T(1024)}, u32[]{:S(2)}) copy-start(f32[2048]{0:T(1024)} %param.11) | copy-start | bytes 24580
  0.7 41.3 %copy-start.5 = (f32[2048]{0:T(1024)S(1)}, f32[2048]{0:T(1024)}, u32[]{:S(2)}) copy-start(f32[2048]{0:T(1024)} %param.10) | copy-start | bytes 24580
  238.2 11.8 %copy-start = (bf16[1024,2048]{1,0:T(8,128)(2,1)S(1)}, bf16[1024,2048]{1,0:T(8,128)(2,1)}, u32[]{:S(2)}) copy-start(bf16[1024,2048]{1,0:T(8,128)(2,1)} %get-tuple-element.13) | copy-start | bytes 12582916
  250.0 2.0 copy-start.1

commit v5 on v4

--- a/solution.py
+++ b/solution.py
@@ -552,9 +552,10 @@
         if n == 0 or n == 2:
             sum_done(n // 2)
     ready(order[-1])
-
-    later = [lambda k=k: sum_done(k) for k in range(2, CHUNKS)]
-    later += [lambda k=k: gather_done(k) for k in range(CHUNKS)]
+    for k in range(2, CHUNKS):
+        sum_done(k)
+
+    later = [lambda k=k: gather_done(k) for k in range(CHUNKS)]
     for i in range(n_chan):
         d, e = i, n_chan - 1 - i
 

time: 253 us -> 252 us (level)
  Pallas kernels: 236 us -> 233 us
    pallas_call x1, Pallas kernels: 150 us -> 147 us  [backward(): pl.pallas_call(functools.partial(backward_kernel, n_sec, n_chan, n_batch)...]
where the time goes in v5:
time: 252 us; the launch traced here: 250 us
  Pallas kernels  233 us (92%)
  other arithmetic  13.5 us (5%)
  local copies, waits for them, and re-layouts  2.74 us (1%)
    pallas_call x1, Pallas kernels, backward(): pl.pallas_call(functools.partial(backward_kernel, n_sec, n_chan, n_batch)...  147 us
    pallas_call x1, Pallas kernels, late_layer(): pl.pallas_call(functools.partial(late_kernel, n_batch), out_shape=(jax.Sh...  45.2 us
    pallas_call x1, Pallas kernels, early_forward(): pl.pallas_call(functools.partial(early_kernel, n_chan, n_batch), out_shap...  40.3 us
    convert_element_type x1, other arithmetic, body(): grad_late = grad_late.astype(jnp.float32)  11.8 us

profile of v5, /device:TPU:19, one launch (start us, length us, event | category | flops | bytes accessed | tf_op | source)
XLA Modules:
  0.0 249.7 jit_solution(9547391021374519890)
XLA Ops:
  0.6 0.0 copy-start.2
  0.6 0.0 copy-start.3
  0.7 0.0 copy-start.4
  0.7 0.0 copy-start.5
  0.7 40.3 %early_forward.1 = (bf16[1024,1024]{1,0:T(8,128)(2,1)}, bf16[1024,2048]{1,0:T(8,128)(2,1)}, f32[8,2048]{1,0:T(8,128)}) custom-call(bf16[256,1024]{1,0:T(8,128)(2,1)} %bitcast.9, bf16[1024,2048]{1,0:T(8,128)(2,1)} %w_ref.2), custom_call_target="tpu_custom_call" | custom-call | tf_op jit(solution)/shard_map/early_forward/pallas_call | solution.py:137
  41.0 0.9 slice_multiply_fusion
  41.9 0.0 copy-done.2
  41.9 0.0 copy-done.3
  41.9 0.0 copy-done.4
  42.0 0.0 copy-done.5
  42.0 0.7 select_maximum_fusion
  42.7 45.2 %late_layer.1 = (bf16[1024,2048]{1,0:T(8,128)(2,1)}, bf16[1024,2048]{1,0:T(8,128)(2,1)}, bf16[1024,2048]{1,0:T(8,128)(2,1)}) custom-call(bf16[1024,2048]{1,0:T(8,128)(2,1)} %get-tuple-element.11.raw_ref.raw_hbm, f32[8,2048]{1,0:T(8,128)} %get-tuple-element.22.vec_ref, f32[8,2048]{1,0:T(8,128)} %get-tuple-element.21.lvec_ref, bf16[2048,2048]{1,0:T(8,128)(2,1)} %w_hbm.1, ...), custom_call_target="tpu_custom_call" | custom-call | tf_op jit(solution)/shard_map/late_layer/pallas_call | solution.py:265
  87.9 147.2 %backward.1 = (bf16[2048,2048]{1,0:T(8,128)(2,1)}, f32[32,2048]{1,0:T(8,128)}) custom-call(bf16[1024,2048]{1,0:T(8,128)(2,1)} %get-tuple-element.14.act_ref, bf16[1024,2048]{1,0:T(8,128)(2,1)} %get-tuple-element.15.gh_ref, f32[8,2048]{1,0:T(8,128)} %get-tuple-element.22.vec_ref, bf16[2048,2048]{1,0:T(8,128)(2,1)} %w_hbm.1, ...), custom_call_target="tpu_custom_call" | custom-call | tf_op jit(solution)/shard_map/backward/pallas_call | solution.py:634
  235.1 0.0 copy-start
  235.2 11.8 %convert_element_type.7 = f32[2048,2048]{1,0:T(8,128)} convert(bf16[2048,2048]{1,0:T(8,128)(2,1)} %get-tuple-element.17) | non-fusion elementwise | flops 4194304 | bytes 25165824 | tf_op jit(solution)/shard_map/convert_element_type | solution.py:684
  247.0 0.0 copy-done
  247.0 0.0 copy-start.1
  247.0 2.0 copy.13
  249.0 0.0 copy-done.1
  249.0 0.7 copy.14
Async XLA Ops:
  0.6 41.3 %copy-start.2 = (f32[2048]{0:T(1024)S(1)}, f32[2048]{0:T(1024)}, u32[]{:S(2)}) copy-start(f32[2048]{0:T(1024)} %param.14) | copy-start | bytes 24580
  0.6 41.3 %copy-start.3 = (f32[2048]{0:T(1024)S(1)}, f32[2048]{0:T(1024)}, u32[]{:S(2)}) copy-start(f32[2048]{0:T(1024)} %param.13) | copy-start | bytes 24580
  0.7 41.3 %copy-start.4 = (f32[2048]{0:T(1024)S(1)}, f32[2048]{0:T(1024)}, u32[]{:S(2)}) copy-start(f32[2048]{0:T(1024)} %param.11) | copy-start | bytes 24580
  0.7 41.3 %copy-start.5 = (f32[2048]{0:T(1024)S(1)}, f32[2048]{0:T(1024)}, u32[]{:S(2)}) copy-start(f32[2048]{0:T(1024)} %param.10) | copy-start | bytes 24580
  235.1 11.8 %copy-start = (bf16[1024,2048]{1,0:T(8,128)(2,1)S(1)}, bf16[1024,2048]{1,0:T(8,128)(2,1)}, u32[]{:S(2)}) copy-start(bf16[1024,2048]{1,0:T(8,128)(2,1)} %get-tuple-element.13) | copy-start | bytes 12582916
  247.0 2.0 copy-start.1
